TPU v7x, 32 devices: a whole 2x2x4 slice. The times are simulated.
32 devices in a mesh: shot: 8 (over y, x, core), rbin: 4 (over z).
Axes of the slice: x: 2, y: 2, z: 4, core: 2. Of those that a mesh axis runs over, the one named last changes fastest.
Arguments:
- local_gathers: bfloat16 [2, 2, 4096, 1024], P(None, None, 'shot', 'rbin'), may hold values from -6 to 6
- recorded_shots: bfloat16 [8, 2, 2, 256, 2048], P('shot', None, None, 'rbin'), may hold values from -0.25 to 0.25
- block_owner: int32 [4], replicated, may hold values from 0 to 7, as said below
- aperture_start: int32 [4096], P('shot'), may hold values from 0 to 1023, as said below
- aperture_end: int32 [4096], P('shot'), may hold values from 1 to 1024
- taper_bin: int32 [1024], P('rbin'), may hold values from 0 to 7
- taper_gain: float32 [8], replicated, may hold values from 0.25 to 1
Outputs:
- multiples: float32 [2, 2048, 2, 4096], P(None, 'rbin', None, 'shot')
Inputs may be any that keep to these rules, and one draw needn't show every extreme that they name: `block_owner`: the 4 entries are distinct. aperture_start < aperture_end for every shot.
All inputs are finite; a program needn't handle non-finite values.
Results may differ from a plain program's by a relative error of at most 0.0029.
Values may be sent and summed in bfloat16 or wider, within the bound.
No kernel may reach another device: no remote copies, remote signals or barrier semaphores. Data moves between devices by JAX's collectives and lax.ppermute only.
A program may use at most 128 MiB of HBM per device.

v0:
```python
import jax
import jax.numpy as jnp
from jax import lax
from jax.sharding import PartitionSpec as P

BLOCKS = 4
EDGE = 64


def from_root(value, axis, source):
    kept = jnp.where(lax.axis_index(axis) == source, value, 0).astype(value.dtype)
    return lax.psum(kept, axis)


def taper_weights(columns, aperture_start, aperture_end, taper_bin, taper_gain):
    inside = (columns[None, :] >= aperture_start[:, None]) & (
        columns[None, :] < aperture_end[:, None]
    )
    distance = jnp.minimum(
        columns[None, :] - aperture_start[:, None], aperture_end[:, None] - 1 - columns[None, :]
    )
    ramped = jnp.minimum((distance + 1).astype(jnp.float32) / EDGE, 1.0)
    labels = jnp.arange(taper_gain.shape[0], dtype=jnp.int32)
    bin_gain = jnp.sum(
        jnp.where(taper_bin[:, None] == labels[None, :], taper_gain[None, :], 0.0), axis=1
    )
    return jnp.where(inside, ramped, 0.0) * bin_gain[None, :]


def complex_rows(real_part, imag_part):
    upper_half = jnp.concatenate([real_part, -imag_part], axis=2)
    lower_half = jnp.concatenate([imag_part, real_part], axis=2)
    return jnp.concatenate([upper_half, lower_half], axis=1)


def per_device(
    local_gathers, recorded_shots, block_owner, aperture_start, aperture_end, taper_bin, taper_gain
):
    frequencies, _, shot_count, point_count = local_gathers.shape
    block_width = point_count // BLOCKS
    column_index = lax.axis_index("rbin")
    first_point = column_index * point_count
    columns = first_point + jnp.arange(point_count, dtype=jnp.int32)
    weight = taper_weights(columns, aperture_start, aperture_end, taper_bin, taper_gain)
    tapered = (local_gathers.astype(jnp.float32) * weight[None, None]).astype(jnp.bfloat16)
    own_slot = recorded_shots[0]
    grouped = tapered.reshape(frequencies, 2, shot_count, BLOCKS, block_width)

    def block_rows(block_index):
        return lax.dynamic_index_in_dim(grouped, block_index, 3, keepdims=False)

    out_columns = own_slot.shape[-1]
    accumulated = jnp.zeros((frequencies, out_columns, 2 * shot_count), jnp.float32)
    for position in range(BLOCKS):
        block_index = jnp.int32(position)
        root_device = block_owner[block_index]
        received = from_root(own_slot, "shot", root_device)
        operand = received.reshape(frequencies, -1, out_columns)

        def product(running, operand=operand, block_index=block_index):
            picked = block_rows(block_index)
            left_side = complex_rows(picked[:, 0], picked[:, 1])
            return running + lax.dot_general(
                operand, left_side, (((1,), (2,)), ((0,), (0,))), preferred_element_type=jnp.float32
            )

        accumulated = product(accumulated)
    accumulated = lax.psum_scatter(accumulated, "rbin", scatter_dimension=1, tiled=True)
    return -accumulated.reshape(frequencies, -1, 2, shot_count)


def solution(mesh):
    in_specs = (
        P(None, None, "shot", "rbin"),
        P("shot", None, None, "rbin", None),
        P(),
        P("shot"),
        P("shot"),
        P("rbin"),
        P(),
    )
    out_specs = P(None, "rbin", None, "shot")
    return jax.shard_map(
        per_device, mesh=mesh, in_specs=in_specs, out_specs=out_specs, check_vma=False
    )
```

profile of v0, /device:TPU:0, one launch (start us, length us, event | category | flops | bytes accessed | tf_op | source)
XLA Modules:
  0.0 451.6 jit_solution(6764496112837825898)
XLA Ops:
  6.5 0.0 copy-start.3
  6.5 0.0 copy-start.5
  6.5 0.0 copy-start.6
  6.5 0.0 copy-start.4
  6.5 0.0 all-reduce.3.cloned.1.call-start
  6.6 1.5 fusion.40
  10.5 2.5 broadcast_select_fusion
  13.0 2.3 copy.21
  15.3 1.3 copy.24
  16.6 1.3 copy.26
  17.9 1.3 copy.28
  19.2 0.0 all-reduce.3.cloned.1.call-update
  19.2 0.0 reduce-scatter.2.cloned.1.call-start
  19.3 0.0 copy-done.3
  19.3 1.5 copy.22
  20.8 0.0 copy-done.5
  20.8 0.0 copy-done.6
  20.8 0.1 select_reduce_fusion
  20.9 0.0 copy-done.4
  20.9 0.3 select_multiply_fusion
  21.2 0.2 multiply_convert_fusion
  21.4 0.1 fusion.39
  21.5 0.3 copy.30
  21.8 0.3 copy.31
  22.1 0.3 copy.32
  22.4 0.3 copy.33
  22.8 0.8 slice_bitcast_fusion.6
  23.7 79.9 %all-reduce.3.cloned.1.call-done = (bf16[2,128,2048]{1,2,0:T(8,128)(2,1)}, bf16[2,128,2048]{1,2,0:T(8,128)(2,1)}, bf16[2,128,2048]{1,2,0:T(8,128)(2,1)}, bf16[2,128,2048]{1,2,0:T(8,128)(2,1)}) async-done(((bf16[2,128,2048]{1,2,0:T(8,128)(2,1)}, bf16[2,128,2048]{1,2,0:T(8,128)(2,1)}, bf16[2,128,2048]{1,2,0:T(8,128)(2,1)}, bf16[2,128,2048]{1,2,0:T(8,128)(2,1)}), (bf16[2,128,2048]{1,2,0:T(8,128)(2,1)}, ...) | async-done | bytes 4194320 | tf_op jit(solution)/shard_map/psum | solution.py:12
  103.7 0.0 copy-start.2
  103.7 0.0 copy-start.1
  103.7 9.6 %fusion = f32[2,2048,1024]{2,1,0:T(8,128)} fusion(bf16[2,128,2048]{1,2,0:T(8,128)(2,1)} %get-tuple-element.6, bf16[2,512,64]{2,1,0:T(8,128)(2,1)} %get-tuple-element.22, bf16[2,512,64]{2,1,0:T(8,128)(2,1)S(1)} %get-tuple-element.21, bf16[2,512,64]{2,1,0:T(8,128)(2,1)S(1)} %fusion.35), kind=kOutput, calls=%fused_computation.6 | convolution fusion | flops 1075838976 | bytes 18219008 | tf_op jit(solution)/shard_map/dot_general | solution.py:63
  113.3 0.0 copy-done.2
  113.3 0.0 copy-start
  113.3 8.2 %fusion.8 = f32[2,2048,1024]{2,1,0:T(8,128)} fusion(bf16[2,128,2048]{1,2,0:T(8,128)(2,1)S(1)} %copy-done.2, bf16[2,512,64]{2,1,0:T(8,128)(2,1)S(1)} %get-tuple-element.20, bf16[2,512,64]{2,1,0:T(8,128)(2,1)S(1)} %get-tuple-element.19, bf16[2,512,64]{2,1,0:T(8,128)(2,1)S(1)} %fusion.36), kind=kOutput, calls=%fused_computation.14 | convolution fusion | flops 1075838976 | bytes 18219008 | tf_op jit(solution)/shard_map/dot_general | solution.py:63
  121.5 0.0 copy-done.1
  121.5 8.1 %fusion.16 = f32[2,2048,1024]{2,1,0:T(8,128)} fusion(bf16[2,128,2048]{1,2,0:T(8,128)(2,1)S(1)} %copy-done.1, bf16[2,512,64]{2,1,0:T(8,128)(2,1)S(1)} %get-tuple-element.24, bf16[2,512,64]{2,1,0:T(8,128)(2,1)S(1)} %get-tuple-element.23, bf16[2,512,64]{2,1,0:T(8,128)(2,1)S(1)} %fusion.37), kind=kOutput, calls=%fused_computation.22 | convolution fusion | flops 1075838976 | bytes 18219008 | tf_op jit(solution)/shard_map/dot_general | solution.py:63
  129.6 0.0 copy-done
  129.6 23.0 %add_add_fusion = f32[2,2048,1024]{2,1,0:T(8,128)} fusion(f32[2,2048,1024]{2,1,0:T(8,128)} %fusion.16, f32[2,2048,1024]{2,1,0:T(8,128)} %fusion, f32[2,2048,1024]{2,1,0:T(8,128)} %fusion.8, bf16[2,128,2048]{1,2,0:T(8,128)(2,1)S(1)} %copy-done, bf16[2,512,64]{2,1,0:T(8,128)(2,1)S(1)} %get-tuple-element.18, bf16[2,512,64]{2,1,0:T(8,128)(2,1)S(1)} %get-tuple-element.17, ...), kind=kOutput, calls=%fused_computation | convolution fusion | flops 1088421888 | bytes 68550656 | tf_op jit(solution)/shard_map/dot_general | solution.py:63
  152.6 0.0 reduce-scatter.2.cloned.1.call-update
  152.7 280.5 %reduce-scatter.2.cloned.1.call-done = f32[2,512,1024]{2,1,0:T(8,128)} async-done(((f32[2,2048,1024]{2,1,0:T(8,128)}), f32[2,512,1024]{2,1,0:T(8,128)}) %reduce-scatter.2.cloned.1.call-update) | async-done | bytes 4194320 | tf_op jit(solution)/shard_map/reduce_scatter | solution.py:68
  433.2 5.0 %neg.22 = f32[2,512,1024]{2,1,0:T(8,128)} negate(f32[2,512,1024]{2,1,0:T(8,128)} %reduce-scatter.2.cloned.1.call-done) | non-fusion elementwise | flops 1048576 | bytes 8388608 | tf_op jit(solution)/shard_map/neg | solution.py:69
  438.2 6.6 %neg.23 = f32[2,512,2,512]{3,2,1,0:T(2,128)} reshape(f32[2,512,1024]{2,1,0:T(8,128)} %neg.22) | data formatting | bytes 8388608 | tf_op jit(solution)/shard_map/neg | solution.py:69
  (9 shorter events, 0.3 us)
Async XLA Ops:
  6.5 12.7 %copy-start.3 = (s32[512]{0:T(512)S(1)}, s32[512]{0:T(512)}, u32[]{:S(2)}) copy-start(s32[512]{0:T(512)} %param.11) | copy-start | bytes 6148
  6.5 14.3 %copy-start.5 = (s32[256]{0:T(256)S(1)}, s32[256]{0:T(256)}, u32[]{:S(2)}) copy-start(s32[256]{0:T(256)} %param.12) | copy-start | bytes 3076
  6.5 14.3 %copy-start.6 = (f32[8]{0:T(128)S(1)}, f32[8]{0:T(128)}, u32[]{:S(2)}) copy-start(f32[8]{0:T(128)} %param.13) | copy-start | bytes 100
  6.5 14.4 %copy-start.4 = (s32[512]{0:T(512)S(1)}, s32[512]{0:T(512)}, u32[]{:S(2)}) copy-start(s32[512]{0:T(512)} %param.10) | copy-start | bytes 6148
  6.5 97.1 %all-reduce.3.cloned.1.call-start = ((), (), s32[]{:S(2)}) async-start(), calls=%async_computation.2 | async-start | bytes 8388608 | tf_op jit(solution)/shard_map/psum | solution.py:12
  19.2 414.0 %reduce-scatter.2.cloned.1.call-start = ((), (), s32[]{:S(2)}) async-start(), calls=%async_computation.1 | async-start | bytes 20971520 | tf_op jit(solution)/shard_map/reduce_scatter | solution.py:68
  103.7 9.7 %copy-start.2 = (bf16[2,128,2048]{1,2,0:T(8,128)(2,1)S(1)}, bf16[2,128,2048]{1,2,0:T(8,128)(2,1)}, u32[]{:S(2)}) copy-start(bf16[2,128,2048]{1,2,0:T(8,128)(2,1)} %get-tuple-element.7) | copy-start | bytes 3145732
  103.7 17.8 %copy-start.1 = (bf16[2,128,2048]{1,2,0:T(8,128)(2,1)S(1)}, bf16[2,128,2048]{1,2,0:T(8,128)(2,1)}, u32[]{:S(2)}) copy-start(bf16[2,128,2048]{1,2,0:T(8,128)(2,1)} %get-tuple-element.5) | copy-start | bytes 3145732
  113.3 16.3 %copy-start = (bf16[2,128,2048]{1,2,0:T(8,128)(2,1)S(1)}, bf16[2,128,2048]{1,2,0:T(8,128)(2,1)}, u32[]{:S(2)}) copy-start(bf16[2,128,2048]{1,2,0:T(8,128)(2,1)} %get-tuple-element.8) | copy-start | bytes 3145732
Sparse Core Ops, SparseCore 0:
  19.3 84.2 all-reduce.2
  152.8 280.3 reduce-scatter.1
where the time goes:
time: 452 us
  waiting for transfers between devices  360 us (80%)
  matrix products  49 us (11%)
  local copies, waits for them, and re-layouts  17.8 us (4%)
  between operations  16 us (4%)
  other arithmetic  8.24 us (2%)
    reduce_scatter x1, waiting for transfers between devices, per_device(): lax.psum_scatter(accumulated, 'rbin', scatter_dimension=1, tiled=True)  281 us
    psum x1, waiting for transfers between devices, from_root(): return lax.psum(kept, axis)  79.9 us
    dot_general x4, matrix products, product(): lax.dot_general(operand, left_side, (((1,), (2,)), ((0,), (0,))), preferr...  49 us
  transfers between devices with their start and end apart: 2, of which 2 were waited for; matrix products, arithmetic and copies ran while one was open for 1% of the time, Pallas kernels for 0%

commit v1 on v0

v1 whole, which is shorter than its diff:
```python
import jax
import jax.numpy as jnp
from jax import lax
from jax.sharding import PartitionSpec as P

BLOCKS = 4
EDGE = 64


def taper_weights(columns, aperture_start, aperture_end, taper_bin, taper_gain):
    inside = (columns[None, :] >= aperture_start[:, None]) & (
        columns[None, :] < aperture_end[:, None]
    )
    distance = jnp.minimum(
        columns[None, :] - aperture_start[:, None], aperture_end[:, None] - 1 - columns[None, :]
    )
    ramped = jnp.minimum((distance + 1).astype(jnp.float32) / EDGE, 1.0)
    labels = jnp.arange(taper_gain.shape[0], dtype=jnp.int32)
    bin_gain = jnp.sum(
        jnp.where(taper_bin[:, None] == labels[None, :], taper_gain[None, :], 0.0), axis=1
    )
    return jnp.where(inside, ramped, 0.0) * bin_gain[None, :]


def per_device(
    local_gathers, recorded_shots, block_owner, aperture_start, aperture_end, taper_bin, taper_gain
):
    freqs, _, shots, points = local_gathers.shape
    rows, receivers = recorded_shots.shape[3:]
    slots = lax.axis_size("shot")
    bins = lax.axis_size("rbin")
    own = receivers // bins
    parts = slots // (2 * freqs)
    part = own // parts

    columns = lax.axis_index("rbin") * points + jnp.arange(points, dtype=jnp.int32)
    weight = taper_weights(columns, aperture_start, aperture_end, taper_bin, taper_gain)
    tapered = (local_gathers.astype(jnp.float32) * -weight[None, None]).astype(jnp.bfloat16)
    gathers = lax.all_gather(tapered, "rbin")

    shares = recorded_shots[0].reshape(freqs, 2, rows, bins, parts, part)
    shares = shares.transpose(0, 1, 4, 3, 2, 5).reshape(slots, bins, rows, part)
    shares = lax.all_to_all(shares, "shot", 0, 0)
    picked = jnp.take(shares, block_owner, axis=0).transpose(1, 0, 2, 3)
    picked = lax.all_to_all(picked, "rbin", 0, 0)
    picked = picked.reshape(bins * BLOCKS * rows, part).T
    recorded = lax.all_gather(picked, "shot").reshape(freqs, 2, own, bins * points)

    real = recorded[:, 0]
    imag = recorded[:, 1]
    g = gathers.transpose(1, 2, 3, 0, 4).reshape(freqs, 2, shots, bins * points)

    def dot(a, b):
        return lax.dot_general(a, b, (((2,), (2,)), ((0,), (0,))), preferred_element_type=jnp.float32)

    out_real = dot(real, g[:, 0]) - dot(imag, g[:, 1])
    out_imag = dot(real, g[:, 1]) + dot(imag, g[:, 0])
    return jnp.stack([out_real, out_imag], axis=2)


def solution(mesh):
    in_specs = (
        P(None, None, "shot", "rbin"),
        P("shot", None, None, "rbin", None),
        P(),
        P("shot"),
        P("shot"),
        P("rbin"),
        P(),
    )
    out_specs = P(None, "rbin", None, "shot")
    return jax.shard_map(
        per_device, mesh=mesh, in_specs=in_specs, out_specs=out_specs, check_vma=False
    )
```

time: 452 us -> 173 us (0.38)
  waiting for transfers between devices: 360 us -> 75.8 us
  matrix products: 49 us -> 9.24 us
  blocking collectives: 0 us -> 33.3 us
  local copies, waits for them, and re-layouts: 17.8 us -> 29.5 us
  starting transfers between devices: 0.08 us -> 5.21 us
    reduce_scatter x1 -> x0, waiting for transfers between devices: 281 us -> none  [per_device(): lax.psum_scatter(accumulated, 'rbin', scatter_dimension=1, tiled=True)]
    psum x1 -> x0, waiting for transfers between devices: 79.9 us -> none  [from_root(): return lax.psum(kept, axis)]
    all_gather x0 -> x2, waiting for transfers between devices: none -> 60.4 us  [the longest x1 37.9 us: per_device(): gathers = lax.all_gather(tapered, 'rbin')]
    dot_general x4, matrix products: 49 us -> 9.24 us  [dot(): lax.dot_general(a, b, (((2,), (2,)), ((0,), (0,))), preferred_element_typ...]
    all_to_all x0 -> x1, blocking collectives: none -> 33.3 us  [per_device(): picked = lax.all_to_all(picked, 'rbin', 0, 0)]
    all_to_all x0 -> x1, waiting for transfers between devices: none -> 15.3 us  [per_device(): shares = lax.all_to_all(shares, 'shot', 0, 0)]
    all_gather x0 -> x2, local copies, waits for them, and re-layouts: none -> 13.8 us  [the longest x1 7.44 us: per_device(): gathers = lax.all_gather(tapered, 'rbin')]
    neg x1 -> x0, local copies, waits for them, and re-layouts: 6.57 us -> none  [per_device(): return -accumulated.reshape(frequencies, -1, 2, shot_count)]
  transfers between devices with their start and end apart: 2 -> 3, of which waited for: 2 -> 3; matrix products, arithmetic and copies ran while one was open for 1% -> 10% of each run, Pallas kernels for 0% -> 0%
where the time goes in v1:
time: 173 us; the launch traced here: 172 us
  waiting for transfers between devices  75.8 us (44%)
  blocking collectives  33.3 us (19%)
  local copies, waits for them, and re-layouts  29.5 us (17%)
  between operations  13.5 us (8%)
  matrix products  9.24 us (5%)
  other arithmetic  5.63 us (3%)
  starting transfers between devices  5.21 us (3%)
    all_gather x1, waiting for transfers between devices, per_device(): gathers = lax.all_gather(tapered, 'rbin')  37.9 us
    all_to_all x1, blocking collectives, per_device(): picked = lax.all_to_all(picked, 'rbin', 0, 0)  33.3 us
    all_gather x1, waiting for transfers between devices, per_device(): lax.all_gather(picked, 'shot').reshape(freqs, 2, own, bins * points)  22.5 us
    all_to_all x1, waiting for transfers between devices, per_device(): shares = lax.all_to_all(shares, 'shot', 0, 0)  15.3 us
    dot_general x4, matrix products, dot(): lax.dot_general(a, b, (((2,), (2,)), ((0,), (0,))), preferred_element_typ...  9.24 us
    reshape x1, local copies, waits for them, and re-layouts, per_device(): g = gathers.transpose(1, 2, 3, 0, 4).reshape(freqs, 2, shots, bins * points)  7.78 us
    all_gather x1, local copies, waits for them, and re-layouts, per_device(): gathers = lax.all_gather(tapered, 'rbin')  7.44 us
    all_gather x1, local copies, waits for them, and re-layouts, per_device(): lax.all_gather(picked, 'shot').reshape(freqs, 2, own, bins * points)  6.39 us
  transfers between devices with their start and end apart: 3, of which 3 were waited for; matrix products, arithmetic and copies ran while one was open for 10% of the time, Pallas kernels for 0%

profile of v1, /device:TPU:0, one launch (start us, length us, event | category | flops | bytes accessed | tf_op | source)
XLA Modules:
  0.0 172.2 jit_solution(5822606526215649655)
XLA Ops:
  6.5 0.0 all-gather.7.cloned.1.call-start
  6.5 0.7 broadcast_add_fusion
  7.2 0.8 select_reduce_fusion
  8.0 0.0 copy-start.2
  8.0 1.1 multiply_negate_fusion
  9.1 2.5 %multiply_convert_fusion = bf16[2,2,512,256]{3,2,1,0:T(8,128)(2,1)} fusion(bf16[2,2,512,256]{3,2,1,0:T(8,128)(2,1)} %param.7, f32[512,256]{1,0:T(8,128)S(1)} %multiply_negate_fusion), kind=kLoop, calls=%fused_computation.9 | loop fusion | flops 1572864 | bytes 2621440 | tf_op jit(solution)/shard_map/convert_element_type | solution.py:38
  11.6 0.0 all-gather.7.cloned.1.call-update
  11.6 0.0 copy-done.2
  11.6 0.8 reshape_squeeze.3
  12.4 0.0 copy-start.3
  12.5 1.2 copy.30
  13.7 5.2 %all-to-all-start = ((bf16[8,4,64,256]{3,2,1,0:T(8,128)(2,1)}), bf16[8,4,64,256]{3,2,1,0:T(8,128)(2,1)S(1)}, u32[]{:S(2)}, u32[]{:S(2)}) async-start(bf16[8,4,64,256]{3,2,1,0:T(8,128)(2,1)} %bitcast.1), calls=%async_computation | async-start | bytes 2097152 | tf_op jit(solution)/shard_map/all_to_all | solution.py:43
  18.8 0.0 all-gather.5.cloned.1.call-start
  18.9 0.0 copy-done.3
  18.9 15.3 %all-to-all-done = bf16[8,4,64,256]{3,2,1,0:T(8,128)(2,1)S(1)} async-done(((bf16[8,4,64,256]{3,2,1,0:T(8,128)(2,1)}), bf16[8,4,64,256]{3,2,1,0:T(8,128)(2,1)S(1)}, u32[]{:S(2)}, u32[]{:S(2)}) %all-to-all-start) | async-done | bytes 1048608 | tf_op jit(solution)/shard_map/all_to_all | solution.py:43
  34.2 0.6 gather_fusion
  34.8 0.1 select_bitcast_fusion
  35.0 33.3 %all_to_all.10 = bf16[4,4,64,256]{3,2,1,0:T(8,128)(2,1)} all-to-all(bf16[4,4,64,256]{3,2,1,0:T(8,128)(2,1)S(1)} %copy.31), channel_id=1, replica_groups=mesh['shot'=8,'rbin'=4] {'rbin'}, dimensions={0} | all-to-all | bytes 1048576 | tf_op jit(solution)/shard_map/all_to_all | solution.py:45
  68.3 0.0 all-gather.5.cloned.1.call-update
  68.4 37.9 %all-gather.7.cloned.1.call-done = bf16[8,2,512,256]{3,2,1,0:T(8,128)(2,1)} async-done(((bf16[2,2,512,256]{3,2,1,0:T(8,128)(2,1)}), bf16[8,2,512,256]{3,2,1,0:T(8,128)(2,1)}) %all-gather.7.cloned.1.call-update) | async-done | bytes 4194320 | tf_op jit(solution)/shard_map/all_gather | solution.py:39
  106.3 7.4 %copy.40 = bf16[4,2,2,512,256]{4,0,3,1,2:T(4,128)(2,1)} copy(bf16[4,2,2,512,256]{4,3,2,1,0:T(8,128)(2,1)} %bitcast.49) | data formatting | bytes 8388608 | tf_op jit(solution)/shard_map/all_gather | solution.py:39
  113.7 7.8 %reshape.154 = bf16[2,2,512,1024]{3,2,0,1:T(8,128)(2,1)} reshape(bf16[2,2,512,4,256]{4,3,2,0,1:T(4,128)(2,1)} %bitcast.48) | data formatting | bytes 8388608 | tf_op jit(solution)/shard_map/reshape | solution.py:51
  121.5 22.5 %all-gather.5.cloned.1.call-done = bf16[2048,1024]{0,1:T(8,128)(2,1)} async-done(((bf16[256,1024]{0,1:T(8,128)(2,1)}), bf16[2048,1024]{0,1:T(8,128)(2,1)}) %all-gather.5.cloned.1.call-update) | async-done | bytes 4194320 | tf_op jit(solution)/shard_map/all_gather | solution.py:47
  144.0 6.4 %copy.32 = bf16[2048,1024]{1,0:T(8,128)(2,1)} copy(bf16[2048,1024]{0,1:T(8,128)(2,1)} %all-gather.5.cloned.1.call-done) | data formatting | bytes 8388608 | tf_op jit(solution)/shard_map/all_gather | solution.py:47
  150.4 0.0 copy-start
  150.4 3.7 %fusion = f32[2,512,512]{2,1,0:T(8,128)S(1)} fusion(bf16[2,2,512,1024]{3,2,1,0:T(8,128)(2,1)} %bitcast.50, bf16[2,2,512,1024]{3,2,0,1:T(8,128)(2,1)} %reshape.154), kind=kOutput, calls=%fused_computation.10 | convolution fusion | flops 1073741824 | bytes 6291456 | tf_op jit(solution)/shard_map/dot_general | solution.py:54
  154.1 0.0 copy-done
  154.1 0.0 copy-start.1
  154.1 3.0 %fusion.1 = f32[2,512,512]{2,1,0:T(8,128)S(1)} fusion(bf16[2,2,512,1024]{3,2,1,0:T(8,128)(2,1)} %bitcast.51, bf16[2,2,512,1024]{3,2,0,1:T(8,128)(2,1)S(1)} %copy-done), kind=kOutput, calls=%fused_computation.11 | convolution fusion | flops 1073741824 | bytes 6291456 | tf_op jit(solution)/shard_map/dot_general | solution.py:54
  157.1 0.0 copy-done.1
  157.1 1.3 add_bitcast_fusion
  158.4 1.3 subtract_bitcast_fusion
  159.7 0.4 pad_maximum_fusion
  160.2 5.2 %copy.36 = f32[2,512,2,512]{3,2,1,0:T(2,128)} copy(f32[2,512,2,512]{3,1,0,2:T(8,128)S(1)} %pad_maximum_fusion) | data formatting | bytes 8388608 | tf_op jit(solution)/shard_map/stack | solution.py:58
  (5 shorter events, 0.1 us)
Async XLA Ops:
  6.5 99.7 %all-gather.7.cloned.1.call-start = ((), (), s32[]{:S(2)}) async-start(), calls=%async_computation.3 | async-start | bytes 5242880 | tf_op jit(solution)/shard_map/all_gather | solution.py:39
  8.0 3.6 %copy-start.2 = (bf16[1,2,2,64,2048]{4,3,2,1,0:T(8,128)(2,1)S(1)}, bf16[1,2,2,64,2048]{4,3,2,1,0:T(8,128)(2,1)}, u32[]{:S(2)}) copy-start(bf16[1,2,2,64,2048]{4,3,2,1,0:T(8,128)(2,1)} %param.8) | copy-start | bytes 3145732
  12.4 6.4 %copy-start.3 = (s32[4]{0:T(128)S(1)}, s32[4]{0:T(128)}, u32[]{:S(2)}) copy-start(s32[4]{0:T(128)} %param.9) | copy-start | bytes 52
  13.7 20.6 %all-to-all-start = ((bf16[8,4,64,256]{3,2,1,0:T(8,128)(2,1)}), bf16[8,4,64,256]{3,2,1,0:T(8,128)(2,1)S(1)}, u32[]{:S(2)}, u32[]{:S(2)}) async-start(bf16[8,4,64,256]{3,2,1,0:T(8,128)(2,1)} %bitcast.1), calls=%async_computation | async-start | bytes 2097152 | tf_op jit(solution)/shard_map/all_to_all | solution.py:43
  18.8 125.2 %all-gather.5.cloned.1.call-start = ((), (), s32[]{:S(2)}) async-start(), calls=%async_computation.2 | async-start | bytes 4718592 | tf_op jit(solution)/shard_map/all_gather | solution.py:47
  150.4 3.7 %copy-start = (bf16[2,2,512,1024]{3,2,0,1:T(8,128)(2,1)S(1)}, bf16[2,2,512,1024]{3,2,0,1:T(8,128)(2,1)}, u32[]{:S(2)}) copy-start(bf16[2,2,512,1024]{3,2,0,1:T(8,128)(2,1)} %reshape.154) | copy-start | bytes 12582916
  154.1 3.0 %copy-start.1 = (bf16[2048,1024]{1,0:T(8,128)(2,1)S(1)}, bf16[2048,1024]{1,0:T(8,128)(2,1)}, u32[]{:S(2)}) copy-start(bf16[2048,1024]{1,0:T(8,128)(2,1)} %copy.32) | copy-start | bytes 12582916
Sparse Core Ops, SparseCore 0:
  11.7 94.4 all-gather.6
  108.2 35.8 all-gather.4

commit v2 on v1

v2 whole, which is shorter than its diff:
```python
import functools

import jax
import jax.numpy as jnp
from jax import lax
from jax.experimental import pallas as pl
from jax.experimental.pallas import tpu as pltpu
from jax.sharding import PartitionSpec as P

BLOCKS = 4
EDGE = 64
ROWS = 256
EARLY_BYTES = 40 * 2**20
LATE_BYTES = 16 * 2**20
ROWS_BY_ROWS = (((1,), (1,)), ((), ()))
WHOLE = pl.BlockSpec(memory_space=pltpu.VMEM)
SCALARS = pl.BlockSpec(memory_space=pltpu.SMEM)
IN_PLACE = pl.BlockSpec(memory_space=pl.ANY)


def exchange(value, axis, distance, among=None):
    pairs = [(i ^ distance, i) for i in range(lax.axis_size(axis))]
    return lax.ppermute(value, axis, [p for p in pairs if among is None or p in among])


def after(value, *earlier):
    return lax.optimization_barrier((value, earlier))[0]


def taper_kernel(first_ref, gain_ref, start_ref, end_ref, bin_ref, origin_ref, gathers_ref, tapered_ref):
    shots, points = gathers_ref.shape[2:]
    origins = origin_ref[...] == lax.broadcasted_iota(jnp.int32, (points, points), 0)
    origins = origins.astype(jnp.float32).astype(jnp.bfloat16)
    labels = bin_ref[...]
    column = first_ref[0] + lax.broadcasted_iota(jnp.int32, labels.shape, 1)
    gain = jnp.zeros(labels.shape, jnp.float32)
    for label in range(gain_ref.shape[0]):
        gain = gain + jnp.where(labels == label, gain_ref[label], 0.0)
    start = jnp.broadcast_to(start_ref[...], (128, shots)).T[:, :1]
    end = jnp.broadcast_to(end_ref[...], (128, shots)).T[:, :1]
    distance = jnp.minimum(column - start, end - 1 - column)
    ramped = jnp.minimum((distance + 1).astype(jnp.float32) / EDGE, 1.0)
    weight = jnp.where(distance >= 0, ramped, 0.0) * -gain
    for freq in range(gathers_ref.shape[0]):
        for part in range(2):
            value = (gathers_ref[freq, part].astype(jnp.float32) * weight).astype(jnp.bfloat16)
            value = jnp.dot(value, origins, preferred_element_type=jnp.float32).astype(jnp.bfloat16)
            tapered_ref[freq, part] = value


def taper(gathers, aperture_start, aperture_end, taper_bin, taper_gain, origin):
    shots, points = gathers.shape[2:]
    first = (lax.axis_index("rbin") * points).reshape(1)
    return pl.pallas_call(
        taper_kernel,
        in_specs=[SCALARS, SCALARS, WHOLE, WHOLE, WHOLE, WHOLE, WHOLE],
        out_specs=WHOLE,
        out_shape=jax.ShapeDtypeStruct(gathers.shape, jnp.bfloat16),
        name="taper",
    )(
        first,
        taper_gain,
        aperture_start.reshape(1, shots),
        aperture_end.reshape(1, shots),
        taper_bin.reshape(1, points),
        origin.reshape(1, points),
        gathers,
    )


def transpose_kernel(me_ref, picked_ref, out_ref):
    bins, blocks, rows, own = picked_ref.shape
    width = blocks * rows
    for unit in range(bins):
        values = picked_ref[lax.bitwise_xor(me_ref[1], unit)].reshape(width, own)
        out_ref[:, unit * width : (unit + 1) * width] = values.T


def unit_product(r0, r1, g):
    def dot(a, b):
        return lax.dot_general(a, b, ROWS_BY_ROWS, preferred_element_type=jnp.float32)

    return dot(r0, g[0]) + dot(-r1, g[1]), dot(r0, g[1]) + dot(r1, g[0])


def choose(rbin, bins, freq, refs):
    values = [ref[freq] if len(ref.shape) == 4 else ref[...] for ref in refs]
    if len(values) == 1:
        return values[0]
    inner = jnp.logical_and(rbin > 0, rbin < bins - 1)
    return jnp.where(inner, values[0], values[1])


def early_kernel(order, n_operands, n_pieces, me_ref, *refs):
    refs = list(refs)
    piece_refs = [refs.pop(0) for _ in range(n_pieces)]
    operands = [refs.pop(0) for _ in range(n_operands)]
    units = [[[operands[i] for i in unit] for unit in of_freq] for of_freq in order]
    out_ref, real_ref, imag_ref, left_ref, held, done, in_sems, out_sems = refs
    shot, rbin = me_ref[0], me_ref[1]
    copies = [
        pltpu.make_async_copy(ref, held.at[lax.bitwise_xor(shot, d)], in_sems.at[d])
        for d, ref in enumerate(piece_refs)
    ]
    for copy in copies:
        copy.start()
    for copy in copies:
        copy.wait()
    freqs = out_ref.shape[0]
    bins = max(len(of_freq) for of_freq in order)
    parts = n_pieces // (2 * freqs)
    own, width = held.shape[1], held.shape[2] // bins

    def recorded(freq, part, here, unit):
        span = slice(unit * width, (unit + 1) * width)
        first = (freq * 2 + part) * parts
        return jnp.concatenate([held[first + h, here, span] for h in range(parts)], axis=1)

    rows = min(own, ROWS)
    leaving = []
    for freq, of_freq in enumerate(units):
        for chunk in range(own // rows):
            here = slice(chunk * rows, (chunk + 1) * rows)
            real = imag = None
            for unit, candidates in enumerate(of_freq):
                g = choose(rbin, bins, freq, candidates)
                r0, r1 = recorded(freq, 0, here, unit), recorded(freq, 1, here, unit)
                a, b = unit_product(r0, r1, g)
                real = a if real is None else real + a
                imag = b if imag is None else imag + b
            if freq < freqs - 1:
                done[freq, here, 0, :] = real
                done[freq, here, 1, :] = imag
                leaving.append(
                    pltpu.make_async_copy(
                        done.at[freq, here], out_ref.at[freq, here], out_sems.at[freq, chunk]
                    )
                )
                leaving[-1].start()
            else:
                real_ref[here] = real
                imag_ref[here] = imag
                for part in range(2):
                    left_ref[part, here] = recorded(freq, part, here, bins - 1)
    for copy in leaving:
        copy.wait()


def late_kernel(bins, n_candidates, me_ref, *refs):
    candidates = refs[:n_candidates]
    real_ref, imag_ref, left_ref, _, out_ref, done, sems = refs[n_candidates:]
    freq = out_ref.shape[0] - 1
    g = choose(me_ref[1], bins, freq, candidates)
    chunks = sems.shape[0]
    rows = real_ref.shape[0] // chunks
    leaving = []
    for chunk in range(chunks):
        here = slice(chunk * rows, (chunk + 1) * rows)
        a, b = unit_product(left_ref[0, here], left_ref[1, here], g)
        done[here, 0, :] = real_ref[here] + a
        done[here, 1, :] = imag_ref[here] + b
        leaving.append(
            pltpu.make_async_copy(done.at[here], out_ref.at[freq, here], sems.at[chunk])
        )
        leaving[-1].start()
    for copy in leaving:
        copy.wait()


def product(me, pieces, gathers):
    freqs, bins = len(gathers), len(gathers[0])
    shots, points = gathers[0][0][0].shape[-2:]
    n_pieces, (own, held_points) = len(pieces), pieces[0].shape
    chunks = own // min(own, ROWS)
    *full, last = gathers
    operands, order = [], []
    for of_freq in [*full, last[:-1]]:
        order.append([])
        for unit in of_freq:
            for value in unit:
                if not any(value is known for known in operands):
                    operands.append(value)
            order[-1].append([[value is o for o in operands].index(True) for value in unit])
    out_type = jax.ShapeDtypeStruct((freqs, own, 2, shots), jnp.float32)
    sum_type = jax.ShapeDtypeStruct((own, shots), jnp.float32)
    out, real, imag, left = pl.pallas_call(
        functools.partial(early_kernel, order, len(operands), n_pieces),
        in_specs=[SCALARS] + [IN_PLACE] * n_pieces + [WHOLE] * len(operands),
        out_specs=[IN_PLACE, WHOLE, WHOLE, WHOLE],
        out_shape=[
            out_type,
            sum_type,
            sum_type,
            jax.ShapeDtypeStruct((2, own, points), jnp.bfloat16),
        ],
        scratch_shapes=[
            pltpu.VMEM((n_pieces, own, held_points), jnp.bfloat16),
            pltpu.VMEM((freqs - 1, own, 2, shots), jnp.float32),
            pltpu.SemaphoreType.DMA((n_pieces,)),
            pltpu.SemaphoreType.DMA((freqs - 1, chunks)),
        ],
        compiler_params=pltpu.CompilerParams(vmem_limit_bytes=EARLY_BYTES),
        name="early",
    )(me, *pieces, *operands)
    n_last = len(last[-1])
    return pl.pallas_call(
        functools.partial(late_kernel, bins, n_last),
        in_specs=[SCALARS] + [WHOLE] * (n_last + 3) + [IN_PLACE],
        out_specs=IN_PLACE,
        out_shape=out_type,
        scratch_shapes=[
            pltpu.VMEM((own, 2, shots), jnp.float32),
            pltpu.SemaphoreType.DMA((chunks,)),
        ],
        input_output_aliases={n_last + 4: 0},
        compiler_params=pltpu.CompilerParams(vmem_limit_bytes=LATE_BYTES),
        name="late",
    )(me, *last[-1], real, imag, left, out)


def per_device(
    local_gathers, recorded_shots, block_owner, aperture_start, aperture_end, taper_bin, taper_gain
):
    freqs, _, shots, points = local_gathers.shape
    rows, receivers = recorded_shots.shape[3:]
    slots = lax.axis_size("shot")
    bins = lax.axis_size("rbin")
    rbin = lax.axis_index("rbin")
    own = receivers // bins
    parts = slots // (2 * freqs)
    width = rows // parts

    shares = lax.all_to_all(recorded_shots[0].reshape(slots, width, receivers), "shot", 0, 0)
    picked = shares[block_owner].reshape(BLOCKS, width, bins, own).transpose(2, 0, 1, 3)

    origin = jnp.arange(points, dtype=jnp.int32).reshape(BLOCKS, parts, width).transpose(1, 0, 2)
    me = jnp.stack([lax.axis_index("shot"), lax.axis_index("rbin")]).astype(jnp.int32)
    tapered = taper(
        local_gathers, aperture_start, aperture_end, taper_bin, taper_gain, origin
    )
    if bins == 4:
        inner, outward = [(1, 2), (2, 1)], [(1, 0), (2, 3)]
        near = exchange(tapered, "rbin", 1)
        across = exchange(tapered, "rbin", 3, inner)
        picked = lax.all_to_all(after(picked, near, across), "rbin", 0, 0)
        second = exchange(across, "rbin", 1, outward)
        gathers = []
        ready, sent = picked, ()
        for freq in range(freqs):
            crossed = exchange(after(near, ready)[freq], "rbin", 3, inner)
            passed = exchange(after(crossed, sent), "rbin", 1, outward)
            gathers.append([[tapered], [near], [crossed, second], [across, passed]])
            ready, sent = crossed, passed
    else:
        picked = lax.all_to_all(picked, "rbin", 0, 0)
        gathers = [[[tapered]] + [[exchange(tapered, "rbin", d)] for d in range(1, bins)]] * freqs

    piece = pl.pallas_call(
        transpose_kernel,
        in_specs=[SCALARS, WHOLE],
        out_specs=WHOLE,
        out_shape=jax.ShapeDtypeStruct((own, bins * BLOCKS * width), jnp.bfloat16),
        name="turn",
    )(me, picked)
    pieces = []
    for d in range(0, slots, 2):
        other = piece if d == 0 else exchange(piece, "shot", d)
        pieces += [other, exchange(other, "shot", 1)]
    return product(me, pieces, gathers)


def solution(mesh):
    in_specs = (
        P(None, None, "shot", "rbin"),
        P("shot", None, None, "rbin", None),
        P(),
        P("shot"),
        P("shot"),
        P("rbin"),
        P(),
    )
    out_specs = P(None, "rbin", None, "shot")
    return jax.shard_map(
        per_device, mesh=mesh, in_specs=in_specs, out_specs=out_specs, check_vma=False
    )
```

time: 173 us -> 113 us (0.65)
  local copies, waits for them, and re-layouts: 29.5 us -> 6.9 us
  waiting for transfers between devices: 75.8 us -> 53.6 us
  blocking collectives: 33.3 us -> 16.5 us
  starting transfers between devices: 5.21 us -> 21.1 us
  between operations: 13.5 us -> 0.16 us
  Pallas kernels: 0 us -> 13.1 us
  matrix products: 9.24 us -> 0 us
  other arithmetic: 5.63 us -> 0.59 us
    all_gather x2 -> x0, waiting for transfers between devices: 60.4 us -> none  [the longest x1 37.9 us: per_device(): gathers = lax.all_gather(tapered, 'rbin')]
    ppermute x0 -> x14, waiting for transfers between devices: none -> 38.2 us  [exchange(): lax.ppermute(value, axis, [p for p in pairs if among is None or p in among])]
    all_to_all x1, blocking collectives: 33.3 us -> 16.5 us  [per_device(): picked = lax.all_to_all(after(picked, near, across), 'rbin', 0, 0)]
    ppermute x0 -> x14, starting transfers between devices: none -> 16.7 us  [exchange(): lax.ppermute(value, axis, [p for p in pairs if among is None or p in among])]
    all_gather x2 -> x0, local copies, waits for them, and re-layouts: 13.8 us -> none  [the longest x1 7.44 us: per_device(): gathers = lax.all_gather(tapered, 'rbin')]
    pallas_call x0 -> x4, Pallas kernels: none -> 13.1 us  [the longest x1 5.58 us: product(): pl.pallas_call(functools.partial(early_kernel, order, len(operands), n_pi...]
    dot_general x4 -> x0, matrix products: 9.24 us -> none  [dot(): lax.dot_general(a, b, (((2,), (2,)), ((0,), (0,))), preferred_element_typ...]
    another operation x2 -> x0, local copies, waits for them, and re-layouts: 6.05 us -> none  [the longest x1 5.25 us: per_device(): return jnp.stack([out_real, out_imag], axis=2)]
  transfers between devices with their start and end apart: 3 -> 15, of which waited for: 3 -> 6; matrix products, arithmetic and copies ran while one was open for 10% -> 4% of each run, Pallas kernels for 0% -> 7%
where the time goes in v2:
time: 113 us; the launch traced here: 112 us
  waiting for transfers between devices  53.6 us (47%)
  starting transfers between devices  21.1 us (19%)
  blocking collectives  16.5 us (15%)
  Pallas kernels  13.1 us (12%)
  local copies, waits for them, and re-layouts  6.9 us (6%)
    ppermute x14, waiting for transfers between devices, exchange(): lax.ppermute(value, axis, [p for p in pairs if among is None or p in among])  38.2 us
    ppermute x14, starting transfers between devices, exchange(): lax.ppermute(value, axis, [p for p in pairs if among is None or p in among])  16.7 us
    all_to_all x1, blocking collectives, per_device(): picked = lax.all_to_all(after(picked, near, across), 'rbin', 0, 0)  16.5 us
    all_to_all x1, waiting for transfers between devices, per_device(): lax.all_to_all(recorded_shots[0].reshape(slots, width, receivers), 'shot'...  15.4 us
    pallas_call x1, Pallas kernels, product(): pl.pallas_call(functools.partial(early_kernel, order, len(operands), n_pi...  5.58 us
    all_to_all x1, starting transfers between devices, per_device(): lax.all_to_all(recorded_shots[0].reshape(slots, width, receivers), 'shot'...  4.37 us
    pallas_call x1, Pallas kernels, taper(): pl.pallas_call(taper_kernel, in_specs=[SCALARS, SCALARS, WHOLE, WHOLE, WH...  3.03 us
    gather x1, local copies, waits for them, and re-layouts, per_device(): shares[block_owner].reshape(BLOCKS, width, bins, own).transpose(2, 0, 1, 3)  2.62 us
  transfers between devices with their start and end apart: 15, of which 6 were waited for; matrix products, arithmetic and copies ran while one was open for 4% of the time, Pallas kernels for 7%

profile of v2, /device:TPU:0, one launch (start us, length us, event | category | flops | bytes accessed | tf_op | source)
XLA Modules:
  0.0 112.0 jit_solution(6874977440337914995)
XLA Ops:
  0.0 0.0 copy-start.3
  0.0 0.7 reshape.86.origin_ref
  0.7 3.0 %taper.1.refs_8_ = bf16[2,2,512,256]{3,2,1,0:T(8,128)(2,1)} custom-call(s32[1]{0:T(128)} %bitcast.2.first_ref, f32[8]{0:T(128)} %gain_ref.1, s32[1,512]{1,0:T(1,128)} %bitcast.21, s32[1,512]{1,0:T(1,128)} %bitcast.22, s32[1,256]{1,0:T(1,128)} %bitcast.23, s32[1,256]{1,0:T(1,128)} %reshape.86.origin_ref, bf16[2,2,512,256]{3,2,1,0:T(8,128)(2,1)} %gathers_ref.1), custom_call_target="tpu_custom_call" | custom-call | tf_op jit(solution)/shard_map/taper/pallas_call | solution.py:54
  3.7 0.7 collective-permute-start
  4.4 5.8 %collective-permute-start.1 = (bf16[2,2,512,256]{3,2,1,0:T(8,128)(2,1)}, bf16[2,2,512,256]{3,2,1,0:T(8,128)(2,1)S(1)}, u32[]{:S(2)}, u32[]{:S(2)}) collective-permute-start(bf16[2,2,512,256]{3,2,1,0:T(8,128)(2,1)} %taper.1.refs_8_), channel_id=1, source_target_pairs={{1,0},{0,1},{3,2},{2,3},{5,4},{4,5},{7,6},{6,7},{9,8},{8,9},{11,10... | collective-permute-start | bytes 3145736 | tf_op jit(solution)/shard_map/ppermute | solution.py:23
  10.3 0.0 copy-start
  10.3 4.4 %all-to-all-start = ((bf16[8,32,2048]{2,1,0:T(8,128)(2,1)}), bf16[8,32,2048]{2,1,0:T(8,128)(2,1)}, u32[]{:S(2)}, u32[]{:S(2)}) async-start(bf16[8,32,2048]{2,1,0:T(8,128)(2,1)} %bitcast.20), calls=%async_computation | async-start | bytes 2097152 | tf_op jit(solution)/shard_map/all_to_all | solution.py:233
  14.7 0.0 copy-done.3
  14.7 15.4 %all-to-all-done = bf16[8,32,2048]{2,1,0:T(8,128)(2,1)} async-done(((bf16[8,32,2048]{2,1,0:T(8,128)(2,1)}), bf16[8,32,2048]{2,1,0:T(8,128)(2,1)}, u32[]{:S(2)}, u32[]{:S(2)}) %all-to-all-start) | async-done | bytes 1048608 | tf_op jit(solution)/shard_map/all_to_all | solution.py:233
  30.1 2.6 %gather_fusion = bf16[4,32,2048]{2,1,0:T(8,128)(2,1)} fusion(bf16[8,32,2048]{2,1,0:T(8,128)(2,1)} %all-to-all-done, s32[1024]{0:T(1024)S(1)} %pad_clamp_fusion), kind=kCustom, calls=%fused_computation | custom fusion | bytes 1048592 | tf_op jit(solution)/shard_map/gather | solution.py:234
  32.7 1.1 copy.12
  33.8 0.0 collective-permute-done.refs_12_.refs_0_
  33.8 0.0 collective-permute-done.1.refs_9_
  33.8 16.5 %all_to_all.10.picked_ref = bf16[4,4,32,512]{3,2,1,0:T(8,128)(2,1)} all-to-all(bf16[4,4,32,512]{3,2,1,0:T(8,128)(2,1)S(1)} %bitcast.18), channel_id=1, replica_groups=mesh['shot'=8,'rbin'=4] {'rbin'}, dimensions={0} | all-to-all | bytes 1048576 | tf_op jit(solution)/shard_map/all_to_all | solution.py:245
  50.3 0.8 slice_bitcast_fusion.1
  51.2 1.4 %collective-permute-start.2 = (bf16[2,512,256]{2,1,0:T(8,128)(2,1)}, bf16[2,512,256]{2,1,0:T(8,128)(2,1)}, u32[]{:S(2)}, u32[]{:S(2)}) collective-permute-start(bf16[2,512,256]{2,1,0:T(8,128)(2,1)} %slice_bitcast_fusion.1), channel_id=1, source_target_pairs={{2,1},{1,2},{6,5},{5,6},{10,9},{9,10},{14,13},{13,14},{18,17},{17,... | collective-permute-start | bytes 1572872 | tf_op jit(solution)/shard_map/ppermute | solution.py:23
  52.6 0.6 pad_add_fusion.me_ref
  53.2 2.1 %turn.1.refs_0_ = bf16[512,512]{1,0:T(8,128)(2,1)} custom-call(s32[2]{0:T(128)} %pad_add_fusion.me_ref, bf16[4,4,32,512]{3,2,1,0:T(8,128)(2,1)} %all_to_all.10.picked_ref), custom_call_target="tpu_custom_call" | custom-call | tf_op jit(solution)/shard_map/turn/pallas_call | solution.py:258
  55.3 1.5 %collective-permute-start.9 = (bf16[512,512]{1,0:T(8,128)(2,1)}, bf16[512,512]{1,0:T(8,128)(2,1)S(1)}, u32[]{:S(2)}, u32[]{:S(2)}) collective-permute-start(bf16[512,512]{1,0:T(8,128)(2,1)} %turn.1.refs_0_), channel_id=1, source_target_pairs={{16,0},{20,4},{24,8},{28,12},{0,16},{4,20},{8,24},{12,28},{17,1},{... | collective-permute-start | bytes 1572872 | tf_op jit(solution)/shard_map/ppermute | solution.py:23
  56.8 1.3 %collective-permute-start.13 = (bf16[2,2,512,256]{3,2,1,0:T(8,128)(2,1)S(1)}, bf16[2,2,512,256]{3,2,1,0:T(8,128)(2,1)S(1)}, u32[]{:S(2)}, u32[]{:S(2)}) collective-permute-start(bf16[2,2,512,256]{3,2,1,0:T(8,128)(2,1)S(1)} %collective-permute-done.refs_12_.refs_0_), channel_id=1, source_target_pairs={{1,0},{2,3},{5,4},{6,7},{9,8},{10,11},{13,12},{14,15},{17,16},{18,... | collective-permute-start | bytes 3145736 | tf_op jit(solution)/shard_map/ppermute | solution.py:23
  58.1 2.1 %collective-permute-start.11 = (bf16[512,512]{1,0:T(8,128)(2,1)}, bf16[512,512]{1,0:T(8,128)(2,1)S(1)}, u32[]{:S(2)}, u32[]{:S(2)}) collective-permute-start(bf16[512,512]{1,0:T(8,128)(2,1)} %turn.1.refs_0_), channel_id=1, source_target_pairs={{24,0},{28,4},{16,8},{20,12},{8,16},{12,20},{0,24},{4,28},{25,1},{... | collective-permute-start | bytes 1572872 | tf_op jit(solution)/shard_map/ppermute | solution.py:23
  60.2 0.0 collective-permute-start.7
  60.2 0.0 collective-permute-done.2.refs_10_
  60.2 0.7 collective-permute-start.3
  60.9 18.3 %collective-permute-done.9.refs_4_ = bf16[512,512]{1,0:T(8,128)(2,1)S(1)} collective-permute-done((bf16[512,512]{1,0:T(8,128)(2,1)}, bf16[512,512]{1,0:T(8,128)(2,1)S(1)}, u32[]{:S(2)}, u32[]{:S(2)}) %collective-permute-start.9) | collective-permute-done | bytes 524320 | tf_op jit(solution)/shard_map/ppermute | solution.py:23
  79.2 1.3 %collective-permute-start.4 = (bf16[2,512,256]{2,1,0:T(8,128)(2,1)}, bf16[2,512,256]{2,1,0:T(8,128)(2,1)S(1)}, u32[]{:S(2)}, u32[]{:S(2)}) collective-permute-start(bf16[2,512,256]{2,1,0:T(8,128)(2,1)} %collective-permute-done.2.refs_10_), channel_id=1, source_target_pairs={{1,0},{2,3},{5,4},{6,7},{9,8},{10,11},{13,12},{14,15},{17,16},{18,... | collective-permute-start | bytes 1572872 | tf_op jit(solution)/shard_map/ppermute | solution.py:23
  80.5 0.0 collective-permute-done.11.refs_6_
  80.5 0.1 collective-permute-start.6
  80.6 1.2 %collective-permute-done.7.refs_2_ = bf16[512,512]{1,0:T(8,128)(2,1)S(1)} collective-permute-done((bf16[512,512]{1,0:T(8,128)(2,1)}, bf16[512,512]{1,0:T(8,128)(2,1)S(1)}, u32[]{:S(2)}, u32[]{:S(2)}) %collective-permute-start.7) | collective-permute-done | bytes 524320 | tf_op jit(solution)/shard_map/ppermute | solution.py:23
  81.8 0.0 collective-permute-start.10
  81.8 0.0 collective-permute-done.3.refs_14_
  81.8 0.5 collective-permute-start.12
  82.3 11.0 %collective-permute-done.4.refs_13_ = bf16[2,512,256]{2,1,0:T(8,128)(2,1)S(1)} collective-permute-done((bf16[2,512,256]{2,1,0:T(8,128)(2,1)}, bf16[2,512,256]{2,1,0:T(8,128)(2,1)S(1)}, u32[]{:S(2)}, u32[]{:S(2)}) %collective-permute-start.4) | collective-permute-done | bytes 524320 | tf_op jit(solution)/shard_map/ppermute | solution.py:23
  93.3 0.0 collective-permute-start.8
  93.3 0.0 collective-permute-done.13.refs_11_
  93.3 1.3 %collective-permute-start.5 = (bf16[2,512,256]{2,1,0:T(8,128)(2,1)S(1)}, bf16[2,512,256]{2,1,0:T(8,128)(2,1)S(1)}, u32[]{:S(2)}, u32[]{:S(2)}) collective-permute-start(bf16[2,512,256]{2,1,0:T(8,128)(2,1)S(1)} %collective-permute-done.3.refs_14_), channel_id=1, source_target_pairs={{1,0},{2,3},{5,4},{6,7},{9,8},{10,11},{13,12},{14,15},{17,16},{18,... | collective-permute-start | bytes 1572872 | tf_op jit(solution)/shard_map/ppermute | solution.py:23
  94.6 0.0 collective-permute-done.6.refs_1_
  94.6 0.0 collective-permute-done.10.refs_5_
  94.6 0.0 collective-permute-done.12.refs_7_
  94.7 0.6 collective-permute-done.8.refs_3_
  95.2 0.0 copy-done
  95.2 0.0 copy-start.1
  95.2 1.0 copy-done.1
  96.3 0.0 copy-start.2
  96.3 0.6 copy-done.2
  96.9 5.6 %early.1 = (f32[2,512,2,512]{3,2,1,0:T(2,128)}, f32[512,512]{1,0:T(8,128)S(1)}, f32[512,512]{1,0:T(8,128)S(1)}, bf16[2,512,256]{2,1,0:T(8,128)(2,1)S(1)}) custom-call(s32[2]{0:T(128)S(1)} %copy-done.2, bf16[512,512]{1,0:T(8,128)(2,1)S(1)} %copy-done.1, bf16[512,512]{1,0:T(8,128)(2,1)S(1)} %collective-permute-done.6.refs_1_, ...), custom_call_target="tpu_custom_call" | custom-call | tf_op jit(solution)/shard_map/early/pallas_call | solution.py:186
  102.5 7.1 %collective-permute-done.5.refs_1_ = bf16[2,512,256]{2,1,0:T(8,128)(2,1)S(1)} collective-permute-done((bf16[2,512,256]{2,1,0:T(8,128)(2,1)S(1)}, bf16[2,512,256]{2,1,0:T(8,128)(2,1)S(1)}, u32[]{:S(2)}, u32[]{:S(2)}) %collective-permute-start.5) | collective-permute-done | bytes 524320 | tf_op jit(solution)/shard_map/ppermute | solution.py:23
  109.6 2.5 %late.1 = f32[2,512,2,512]{3,2,1,0:T(2,128)} custom-call(s32[2]{0:T(128)S(1)} %copy-done.2, bf16[2,2,512,256]{3,2,1,0:T(8,128)(2,1)S(1)} %collective-permute-done.refs_12_.refs_0_, bf16[2,512,256]{2,1,0:T(8,128)(2,1)S(1)} %collective-permute-done.5.refs_1_, f32[512,512]{1,0:T(8,128)S(1)} %get-tuple-element.17.refs_2_, ...), custom_call_target="tpu_custom_call", output_to_operand_aliasing={{}: (6, {})} | custom-call | tf_op jit(solution)/shard_map/late/pallas_call | solution.py:206
  (4 shorter events, 0.1 us)
Async XLA Ops:
  0.0 14.7 %copy-start.3 = (s32[4]{0:T(128)S(1)}, s32[4]{0:T(128)}, u32[]{:S(2)}) copy-start(s32[4]{0:T(128)} %param.9) | copy-start | bytes 52
  3.7 30.1 %collective-permute-start = (bf16[2,2,512,256]{3,2,1,0:T(8,128)(2,1)}, bf16[2,2,512,256]{3,2,1,0:T(8,128)(2,1)S(1)}, u32[]{:S(2)}, u32[]{:S(2)}) collective-permute-start(bf16[2,2,512,256]{3,2,1,0:T(8,128)(2,1)} %taper.1.refs_8_), channel_id=1, source_target_pairs={{2,1},{1,2},{6,5},{5,6},{10,9},{9,10},{14,13},{13,14},{18,17},{17,... | collective-permute-start | bytes 3145736 | tf_op jit(solution)/shard_map/ppermute | solution.py:23
  4.4 29.4 %collective-permute-start.1 = (bf16[2,2,512,256]{3,2,1,0:T(8,128)(2,1)}, bf16[2,2,512,256]{3,2,1,0:T(8,128)(2,1)S(1)}, u32[]{:S(2)}, u32[]{:S(2)}) collective-permute-start(bf16[2,2,512,256]{3,2,1,0:T(8,128)(2,1)} %taper.1.refs_8_), channel_id=1, source_target_pairs={{1,0},{0,1},{3,2},{2,3},{5,4},{4,5},{7,6},{6,7},{9,8},{8,9},{11,10... | collective-permute-start | bytes 3145736 | tf_op jit(solution)/shard_map/ppermute | solution.py:23
  10.3 85.0 %copy-start = (bf16[2,2,512,256]{3,2,1,0:T(8,128)(2,1)S(1)}, bf16[2,2,512,256]{3,2,1,0:T(8,128)(2,1)}, u32[]{:S(2)}) copy-start(bf16[2,2,512,256]{3,2,1,0:T(8,128)(2,1)} %taper.1.refs_8_) | copy-start | bytes 3145732
  10.3 19.8 %all-to-all-start = ((bf16[8,32,2048]{2,1,0:T(8,128)(2,1)}), bf16[8,32,2048]{2,1,0:T(8,128)(2,1)}, u32[]{:S(2)}, u32[]{:S(2)}) async-start(bf16[8,32,2048]{2,1,0:T(8,128)(2,1)} %bitcast.20), calls=%async_computation | async-start | bytes 2097152 | tf_op jit(solution)/shard_map/all_to_all | solution.py:233
  51.2 9.0 %collective-permute-start.2 = (bf16[2,512,256]{2,1,0:T(8,128)(2,1)}, bf16[2,512,256]{2,1,0:T(8,128)(2,1)}, u32[]{:S(2)}, u32[]{:S(2)}) collective-permute-start(bf16[2,512,256]{2,1,0:T(8,128)(2,1)} %slice_bitcast_fusion.1), channel_id=1, source_target_pairs={{2,1},{1,2},{6,5},{5,6},{10,9},{9,10},{14,13},{13,14},{18,17},{17,... | collective-permute-start | bytes 1572872 | tf_op jit(solution)/shard_map/ppermute | solution.py:23
  55.3 23.9 %collective-permute-start.9 = (bf16[512,512]{1,0:T(8,128)(2,1)}, bf16[512,512]{1,0:T(8,128)(2,1)S(1)}, u32[]{:S(2)}, u32[]{:S(2)}) collective-permute-start(bf16[512,512]{1,0:T(8,128)(2,1)} %turn.1.refs_0_), channel_id=1, source_target_pairs={{16,0},{20,4},{24,8},{28,12},{0,16},{4,20},{8,24},{12,28},{17,1},{... | collective-permute-start | bytes 1572872 | tf_op jit(solution)/shard_map/ppermute | solution.py:23
  56.8 36.5 %collective-permute-start.13 = (bf16[2,2,512,256]{3,2,1,0:T(8,128)(2,1)S(1)}, bf16[2,2,512,256]{3,2,1,0:T(8,128)(2,1)S(1)}, u32[]{:S(2)}, u32[]{:S(2)}) collective-permute-start(bf16[2,2,512,256]{3,2,1,0:T(8,128)(2,1)S(1)} %collective-permute-done.refs_12_.refs_0_), channel_id=1, source_target_pairs={{1,0},{2,3},{5,4},{6,7},{9,8},{10,11},{13,12},{14,15},{17,16},{18,... | collective-permute-start | bytes 3145736 | tf_op jit(solution)/shard_map/ppermute | solution.py:23
  58.1 22.4 %collective-permute-start.11 = (bf16[512,512]{1,0:T(8,128)(2,1)}, bf16[512,512]{1,0:T(8,128)(2,1)S(1)}, u32[]{:S(2)}, u32[]{:S(2)}) collective-permute-start(bf16[512,512]{1,0:T(8,128)(2,1)} %turn.1.refs_0_), channel_id=1, source_target_pairs={{24,0},{28,4},{16,8},{20,12},{8,16},{12,20},{0,24},{4,28},{25,1},{... | collective-permute-start | bytes 1572872 | tf_op jit(solution)/shard_map/ppermute | solution.py:23
  60.2 21.6 %collective-permute-start.7 = (bf16[512,512]{1,0:T(8,128)(2,1)}, bf16[512,512]{1,0:T(8,128)(2,1)S(1)}, u32[]{:S(2)}, u32[]{:S(2)}) collective-permute-start(bf16[512,512]{1,0:T(8,128)(2,1)} %turn.1.refs_0_), channel_id=1, source_target_pairs={{8,0},{12,4},{0,8},{4,12},{24,16},{28,20},{16,24},{20,28},{9,1},{1... | collective-permute-start | bytes 1572872 | tf_op jit(solution)/shard_map/ppermute | solution.py:23
  60.2 21.6 %collective-permute-start.3 = (bf16[2,512,256]{2,1,0:T(8,128)(2,1)S(1)}, bf16[2,512,256]{2,1,0:T(8,128)(2,1)S(1)}, u32[]{:S(2)}, u32[]{:S(2)}) collective-permute-start(bf16[2,512,256]{2,1,0:T(8,128)(2,1)S(1)} %slice_bitcast_fusion), channel_id=1, source_target_pairs={{2,1},{1,2},{6,5},{5,6},{10,9},{9,10},{14,13},{13,14},{18,17},{17,... | collective-permute-start | bytes 1572872 | tf_op jit(solution)/shard_map/ppermute | solution.py:23
  79.2 14.1 %collective-permute-start.4 = (bf16[2,512,256]{2,1,0:T(8,128)(2,1)}, bf16[2,512,256]{2,1,0:T(8,128)(2,1)S(1)}, u32[]{:S(2)}, u32[]{:S(2)}) collective-permute-start(bf16[2,512,256]{2,1,0:T(8,128)(2,1)} %collective-permute-done.2.refs_10_), channel_id=1, source_target_pairs={{1,0},{2,3},{5,4},{6,7},{9,8},{10,11},{13,12},{14,15},{17,16},{18,... | collective-permute-start | bytes 1572872 | tf_op jit(solution)/shard_map/ppermute | solution.py:23
  80.5 14.1 %collective-permute-start.6 = (bf16[512,512]{1,0:T(8,128)(2,1)}, bf16[512,512]{1,0:T(8,128)(2,1)S(1)}, u32[]{:S(2)}, u32[]{:S(2)}) collective-permute-start(bf16[512,512]{1,0:T(8,128)(2,1)} %turn.1.refs_0_), channel_id=1, source_target_pairs={{4,0},{0,4},{12,8},{8,12},{20,16},{16,20},{28,24},{24,28},{5,1},{1... | collective-permute-start | bytes 1572872 | tf_op jit(solution)/shard_map/ppermute | solution.py:23
  81.8 12.9 %collective-permute-start.10 = (bf16[512,512]{1,0:T(8,128)(2,1)S(1)}, bf16[512,512]{1,0:T(8,128)(2,1)S(1)}, u32[]{:S(2)}, u32[]{:S(2)}) collective-permute-start(bf16[512,512]{1,0:T(8,128)(2,1)S(1)} %collective-permute-done.9.refs_4_), channel_id=1, source_target_pairs={{4,0},{0,4},{12,8},{8,12},{20,16},{16,20},{28,24},{24,28},{5,1},{1... | collective-permute-start | bytes 1572872 | tf_op jit(solution)/shard_map/ppermute | solution.py:23
  81.8 12.9 %collective-permute-start.12 = (bf16[512,512]{1,0:T(8,128)(2,1)S(1)}, bf16[512,512]{1,0:T(8,128)(2,1)S(1)}, u32[]{:S(2)}, u32[]{:S(2)}) collective-permute-start(bf16[512,512]{1,0:T(8,128)(2,1)S(1)} %collective-permute-done.11.refs_6_), channel_id=1, source_target_pairs={{4,0},{0,4},{12,8},{8,12},{20,16},{16,20},{28,24},{24,28},{5,1},{1... | collective-permute-start | bytes 1572872 | tf_op jit(solution)/shard_map/ppermute | solution.py:23
  93.3 1.9 %collective-permute-start.8 = (bf16[512,512]{1,0:T(8,128)(2,1)S(1)}, bf16[512,512]{1,0:T(8,128)(2,1)S(1)}, u32[]{:S(2)}, u32[]{:S(2)}) collective-permute-start(bf16[512,512]{1,0:T(8,128)(2,1)S(1)} %collective-permute-done.7.refs_2_), channel_id=1, source_target_pairs={{4,0},{0,4},{12,8},{8,12},{20,16},{16,20},{28,24},{24,28},{5,1},{1... | collective-permute-start | bytes 1572872 | tf_op jit(solution)/shard_map/ppermute | solution.py:23
  93.3 16.2 %collective-permute-start.5 = (bf16[2,512,256]{2,1,0:T(8,128)(2,1)S(1)}, bf16[2,512,256]{2,1,0:T(8,128)(2,1)S(1)}, u32[]{:S(2)}, u32[]{:S(2)}) collective-permute-start(bf16[2,512,256]{2,1,0:T(8,128)(2,1)S(1)} %collective-permute-done.3.refs_14_), channel_id=1, source_target_pairs={{1,0},{2,3},{5,4},{6,7},{9,8},{10,11},{13,12},{14,15},{17,16},{18,... | collective-permute-start | bytes 1572872 | tf_op jit(solution)/shard_map/ppermute | solution.py:23
  95.2 1.0 copy-start.1
  96.3 0.6 copy-start.2

commit v3 on v2

--- a/solution.py
+++ b/solution.py
@@ -2,6 +2,7 @@
 
 import jax
 import jax.numpy as jnp
+import numpy as np
 from jax import lax
 from jax.experimental import pallas as pl
 from jax.experimental.pallas import tpu as pltpu
@@ -10,6 +11,8 @@
 BLOCKS = 4
 EDGE = 64
 ROWS = 256
+PICK_FLOPS = 2 * 10**10
+EARLY_FLOPS = 4 * 10**9
 EARLY_BYTES = 40 * 2**20
 LATE_BYTES = 16 * 2**20
 ROWS_BY_ROWS = (((1,), (1,)), ((), ()))
@@ -23,16 +26,21 @@
     return lax.ppermute(value, axis, [p for p in pairs if among is None or p in among])
 
 
+def cost(flops):
+    return pl.CostEstimate(flops=flops, bytes_accessed=2**21, transcendentals=0)
+
+
 def after(value, *earlier):
     return lax.optimization_barrier((value, earlier))[0]
 
 
-def taper_kernel(first_ref, gain_ref, start_ref, end_ref, bin_ref, origin_ref, gathers_ref, tapered_ref):
+def taper_kernel(gain_ref, start_ref, end_ref, bin_ref, origin_ref, gathers_ref, tapered_ref):
     shots, points = gathers_ref.shape[2:]
     origins = origin_ref[...] == lax.broadcasted_iota(jnp.int32, (points, points), 0)
     origins = origins.astype(jnp.float32).astype(jnp.bfloat16)
     labels = bin_ref[...]
-    column = first_ref[0] + lax.broadcasted_iota(jnp.int32, labels.shape, 1)
+    first = lax.axis_index("rbin") * points
+    column = first + lax.broadcasted_iota(jnp.int32, labels.shape, 1)
     gain = jnp.zeros(labels.shape, jnp.float32)
     for label in range(gain_ref.shape[0]):
         gain = gain + jnp.where(labels == label, gain_ref[label], 0.0)
@@ -50,15 +58,13 @@
 
 def taper(gathers, aperture_start, aperture_end, taper_bin, taper_gain, origin):
     shots, points = gathers.shape[2:]
-    first = (lax.axis_index("rbin") * points).reshape(1)
     return pl.pallas_call(
         taper_kernel,
-        in_specs=[SCALARS, SCALARS, WHOLE, WHOLE, WHOLE, WHOLE, WHOLE],
+        in_specs=[SCALARS, WHOLE, WHOLE, WHOLE, WHOLE, WHOLE],
         out_specs=WHOLE,
         out_shape=jax.ShapeDtypeStruct(gathers.shape, jnp.bfloat16),
         name="taper",
     )(
-        first,
         taper_gain,
         aperture_start.reshape(1, shots),
         aperture_end.reshape(1, shots),
@@ -68,11 +74,31 @@
     )
 
 
-def transpose_kernel(me_ref, picked_ref, out_ref):
+def pick_kernel(owner_ref, shares_ref, picked_ref):
+    bins, blocks, _, own = picked_ref.shape
+    for block in range(blocks):
+        for unit in range(bins):
+            span = slice(unit * own, (unit + 1) * own)
+            picked_ref[unit, block] = shares_ref[owner_ref[block], :, span]
+
+
+def pick(shares, block_owner, bins):
+    _, width, receivers = shares.shape
+    return pl.pallas_call(
+        pick_kernel,
+        in_specs=[SCALARS, WHOLE],
+        out_specs=WHOLE,
+        out_shape=jax.ShapeDtypeStruct((bins, BLOCKS, width, receivers // bins), jnp.bfloat16),
+        cost_estimate=cost(PICK_FLOPS),
+        name="pick",
+    )(block_owner, shares)
+
+
+def transpose_kernel(picked_ref, out_ref):
     bins, blocks, rows, own = picked_ref.shape
     width = blocks * rows
     for unit in range(bins):
-        values = picked_ref[lax.bitwise_xor(me_ref[1], unit)].reshape(width, own)
+        values = picked_ref[lax.bitwise_xor(lax.axis_index("rbin"), unit)].reshape(width, own)
         out_ref[:, unit * width : (unit + 1) * width] = values.T
 
 
@@ -91,13 +117,13 @@
     return jnp.where(inner, values[0], values[1])
 
 
-def early_kernel(order, n_operands, n_pieces, me_ref, *refs):
+def early_kernel(order, n_operands, n_pieces, *refs):
     refs = list(refs)
     piece_refs = [refs.pop(0) for _ in range(n_pieces)]
     operands = [refs.pop(0) for _ in range(n_operands)]
     units = [[[operands[i] for i in unit] for unit in of_freq] for of_freq in order]
     out_ref, real_ref, imag_ref, left_ref, held, done, in_sems, out_sems = refs
-    shot, rbin = me_ref[0], me_ref[1]
+    shot, rbin = lax.axis_index("shot"), lax.axis_index("rbin")
     copies = [
         pltpu.make_async_copy(ref, held.at[lax.bitwise_xor(shot, d)], in_sems.at[d])
         for d, ref in enumerate(piece_refs)
@@ -146,11 +172,11 @@
         copy.wait()
 
 
-def late_kernel(bins, n_candidates, me_ref, *refs):
+def late_kernel(bins, n_candidates, *refs):
     candidates = refs[:n_candidates]
     real_ref, imag_ref, left_ref, _, out_ref, done, sems = refs[n_candidates:]
     freq = out_ref.shape[0] - 1
-    g = choose(me_ref[1], bins, freq, candidates)
+    g = choose(lax.axis_index("rbin"), bins, freq, candidates)
     chunks = sems.shape[0]
     rows = real_ref.shape[0] // chunks
     leaving = []
@@ -167,7 +193,7 @@
         copy.wait()
 
 
-def product(me, pieces, gathers):
+def product(pieces, gathers):
     freqs, bins = len(gathers), len(gathers[0])
     shots, points = gathers[0][0][0].shape[-2:]
     n_pieces, (own, held_points) = len(pieces), pieces[0].shape
@@ -185,7 +211,7 @@
     sum_type = jax.ShapeDtypeStruct((own, shots), jnp.float32)
     out, real, imag, left = pl.pallas_call(
         functools.partial(early_kernel, order, len(operands), n_pieces),
-        in_specs=[SCALARS] + [IN_PLACE] * n_pieces + [WHOLE] * len(operands),
+        in_specs=[IN_PLACE] * n_pieces + [WHOLE] * len(operands),
         out_specs=[IN_PLACE, WHOLE, WHOLE, WHOLE],
         out_shape=[
             out_type,
@@ -200,22 +226,23 @@
             pltpu.SemaphoreType.DMA((freqs - 1, chunks)),
         ],
         compiler_params=pltpu.CompilerParams(vmem_limit_bytes=EARLY_BYTES),
+        cost_estimate=cost(EARLY_FLOPS),
         name="early",
-    )(me, *pieces, *operands)
+    )(*pieces, *operands)
     n_last = len(last[-1])
     return pl.pallas_call(
         functools.partial(late_kernel, bins, n_last),
-        in_specs=[SCALARS] + [WHOLE] * (n_last + 3) + [IN_PLACE],
+        in_specs=[WHOLE] * (n_last + 3) + [IN_PLACE],
         out_specs=IN_PLACE,
         out_shape=out_type,
         scratch_shapes=[
             pltpu.VMEM((own, 2, shots), jnp.float32),
             pltpu.SemaphoreType.DMA((chunks,)),
         ],
-        input_output_aliases={n_last + 4: 0},
+        input_output_aliases={n_last + 3: 0},
         compiler_params=pltpu.CompilerParams(vmem_limit_bytes=LATE_BYTES),
         name="late",
-    )(me, *last[-1], real, imag, left, out)
+    )(*last[-1], real, imag, left, out)
 
 
 def per_device(
@@ -231,10 +258,9 @@
     width = rows // parts
 
     shares = lax.all_to_all(recorded_shots[0].reshape(slots, width, receivers), "shot", 0, 0)
-    picked = shares[block_owner].reshape(BLOCKS, width, bins, own).transpose(2, 0, 1, 3)
-
-    origin = jnp.arange(points, dtype=jnp.int32).reshape(BLOCKS, parts, width).transpose(1, 0, 2)
-    me = jnp.stack([lax.axis_index("shot"), lax.axis_index("rbin")]).astype(jnp.int32)
+    picked = pick(shares, block_owner, bins)
+
+    origin = np.arange(points, dtype=np.int32).reshape(BLOCKS, parts, width).transpose(1, 0, 2)
     tapered = taper(
         local_gathers, aperture_start, aperture_end, taper_bin, taper_gain, origin
     )
@@ -242,12 +268,12 @@
         inner, outward = [(1, 2), (2, 1)], [(1, 0), (2, 3)]
         near = exchange(tapered, "rbin", 1)
         across = exchange(tapered, "rbin", 3, inner)
-        picked = lax.all_to_all(after(picked, near, across), "rbin", 0, 0)
+        picked = lax.all_to_all(picked, "rbin", 0, 0)
         second = exchange(across, "rbin", 1, outward)
         gathers = []
-        ready, sent = picked, ()
+        ready, sent = picked, second
         for freq in range(freqs):
-            crossed = exchange(after(near, ready)[freq], "rbin", 3, inner)
+            crossed = exchange(after(near[freq], ready), "rbin", 3, inner)
             passed = exchange(after(crossed, sent), "rbin", 1, outward)
             gathers.append([[tapered], [near], [crossed, second], [across, passed]])
             ready, sent = crossed, passed
@@ -257,16 +283,16 @@
 
     piece = pl.pallas_call(
         transpose_kernel,
-        in_specs=[SCALARS, WHOLE],
+        in_specs=[WHOLE],
         out_specs=WHOLE,
         out_shape=jax.ShapeDtypeStruct((own, bins * BLOCKS * width), jnp.bfloat16),
         name="turn",
-    )(me, picked)
+    )(picked)
     pieces = []
     for d in range(0, slots, 2):
         other = piece if d == 0 else exchange(piece, "shot", d)
         pieces += [other, exchange(other, "shot", 1)]
-    return product(me, pieces, gathers)
+    return product(pieces, gathers)
 
 
 def solution(mesh):

time: 113 us -> 98 us (0.87)
  blocking collectives: 16.5 us -> 0 us
  local copies, waits for them, and re-layouts: 6.9 us -> 3.09 us
  waiting for transfers between devices: 53.6 us -> 56.5 us
  Pallas kernels: 13.1 us -> 15.2 us
  starting transfers between devices: 21.1 us -> 22.6 us
    all_to_all x1 -> x0, blocking collectives: 16.5 us -> none  [per_device(): picked = lax.all_to_all(after(picked, near, across), 'rbin', 0, 0)]
    all_to_all x0 -> x1, waiting for transfers between devices: none -> 14 us  [per_device(): picked = lax.all_to_all(picked, 'rbin', 0, 0)]
    ppermute x14, waiting for transfers between devices: 38.2 us -> 32.3 us  [exchange(): lax.ppermute(value, axis, [p for p in pairs if among is None or p in among])]
    all_to_all x1, waiting for transfers between devices: 15.4 us -> 10.1 us  [per_device(): lax.all_to_all(recorded_shots[0].reshape(slots, width, receivers), 'shot'...]
    all_to_all x0 -> x1, starting transfers between devices: none -> 5 us  [per_device(): picked = lax.all_to_all(picked, 'rbin', 0, 0)]
    ppermute x14, starting transfers between devices: 16.7 us -> 12.4 us  [exchange(): lax.ppermute(value, axis, [p for p in pairs if among is None or p in among])]
    gather x1 -> x0, local copies, waits for them, and re-layouts: 2.62 us -> none  [per_device(): shares[block_owner].reshape(BLOCKS, width, bins, own).transpose(2, 0, 1, 3)]
    reshape x2 -> x0, local copies, waits for them, and re-layouts: 1.76 us -> none  [the longest x1 1.08 us: per_device(): shares[block_owner].reshape(BLOCKS, width, bins, own).transpose(2, 0, 1, 3)]
  transfers between devices with their start and end apart: 15 -> 16, of which waited for: 6 -> 7; matrix products, arithmetic and copies ran while one was open for 4% -> 1% of each run, Pallas kernels for 7% -> 14%
where the time goes in v3:
time: 98 us; the launch traced here: 97.5 us
  waiting for transfers between devices  56.5 us (58%)
  starting transfers between devices  22.6 us (23%)
  Pallas kernels  15.2 us (16%)
  local copies, waits for them, and re-layouts  3.09 us (3%)
    ppermute x14, waiting for transfers between devices, exchange(): lax.ppermute(value, axis, [p for p in pairs if among is None or p in among])  32.3 us
    all_to_all x1, waiting for transfers between devices, per_device(): picked = lax.all_to_all(picked, 'rbin', 0, 0)  14 us
    ppermute x14, starting transfers between devices, exchange(): lax.ppermute(value, axis, [p for p in pairs if among is None or p in among])  12.4 us
    all_to_all x1, waiting for transfers between devices, per_device(): lax.all_to_all(recorded_shots[0].reshape(slots, width, receivers), 'shot'...  10.1 us
    pallas_call x1, Pallas kernels, product(): pl.pallas_call(functools.partial(early_kernel, order, len(operands), n_pi...  6.13 us
    all_to_all x1, starting transfers between devices, per_device(): lax.all_to_all(recorded_shots[0].reshape(slots, width, receivers), 'shot'...  5.17 us
    all_to_all x1, starting transfers between devices, per_device(): picked = lax.all_to_all(picked, 'rbin', 0, 0)  5 us
    pallas_call x1, Pallas kernels, taper(): pl.pallas_call(taper_kernel, in_specs=[SCALARS, WHOLE, WHOLE, WHOLE, WHOL...  3.04 us
  transfers between devices with their start and end apart: 16, of which 7 were waited for; matrix products, arithmetic and copies ran while one was open for 1% of the time, Pallas kernels for 14%

profile of v3, /device:TPU:0, one launch (start us, length us, event | category | flops | bytes accessed | tf_op | source)
XLA Modules:
  0.0 97.5 jit_solution(11727684949786907308)
XLA Ops:
  0.0 5.2 %all-to-all-start = ((bf16[8,32,2048]{2,1,0:T(8,128)(2,1)}), bf16[8,32,2048]{2,1,0:T(8,128)(2,1)S(1)}, u32[]{:S(2)}, u32[]{:S(2)}) async-start(bf16[8,32,2048]{2,1,0:T(8,128)(2,1)} %bitcast.8), calls=%async_computation | async-start | bytes 2097152 | tf_op jit(solution)/shard_map/all_to_all | solution.py:260
  5.2 3.0 %taper.1.refs_8_ = bf16[2,2,512,256]{3,2,1,0:T(8,128)(2,1)} custom-call(f32[8]{0:T(128)} %gain_ref.1, s32[1,512]{1,0:T(1,128)} %bitcast.9, s32[1,512]{1,0:T(1,128)} %bitcast.10, s32[1,256]{1,0:T(1,128)} %bitcast.11, s32[1,256]{1,0:T(1,128)} %constant.2.clone.origin_ref, bf16[2,2,512,256]{3,2,1,0:T(8,128)(2,1)} %gathers_ref.1), custom_call_target="tpu_custom_call" | custom-call | tf_op jit(solution)/shard_map/taper/pallas_call | solution.py:61
  8.2 1.6 %collective-permute-start.1 = (bf16[2,2,512,256]{3,2,1,0:T(8,128)(2,1)}, bf16[2,2,512,256]{3,2,1,0:T(8,128)(2,1)S(1)}, u32[]{:S(2)}, u32[]{:S(2)}) collective-permute-start(bf16[2,2,512,256]{3,2,1,0:T(8,128)(2,1)} %taper.1.refs_8_), channel_id=1, source_target_pairs={{1,0},{0,1},{3,2},{2,3},{5,4},{4,5},{7,6},{6,7},{9,8},{8,9},{11,10... | collective-permute-start | bytes 3145736 | tf_op jit(solution)/shard_map/ppermute | solution.py:26
  9.8 0.7 collective-permute-start
  10.5 10.1 %all-to-all-done.shares_ref = bf16[8,32,2048]{2,1,0:T(8,128)(2,1)S(1)} async-done(((bf16[8,32,2048]{2,1,0:T(8,128)(2,1)}), bf16[8,32,2048]{2,1,0:T(8,128)(2,1)S(1)}, u32[]{:S(2)}, u32[]{:S(2)}) %all-to-all-start) | async-done | bytes 1048608 | tf_op jit(solution)/shard_map/all_to_all | solution.py:260
  20.6 0.0 copy-start.2
  20.6 1.0 %copy-done.2 = bf16[8,32,2048]{2,1,0:T(8,128)(2,1)} copy-done((bf16[8,32,2048]{2,1,0:T(8,128)(2,1)}, bf16[8,32,2048]{2,1,0:T(8,128)(2,1)S(1)}, u32[]{:S(2)}) %copy-start.2) | copy-done | bytes 1048600
  21.6 2.1 %pick.1 = bf16[4,4,32,512]{3,2,1,0:T(8,128)(2,1)} custom-call(s32[4]{0:T(128)} %owner_ref.1, bf16[8,32,2048]{2,1,0:T(8,128)(2,1)} %copy-done.2), custom_call_target="tpu_custom_call" | custom-call | flops 20000000000 | bytes 2097152 | tf_op jit(solution)/shard_map/pick/pallas_call | solution.py:87
  23.7 0.0 copy-start
  23.7 5.0 %all-to-all-start.1 = ((bf16[4,4,32,512]{3,2,1,0:T(8,128)(2,1)}), bf16[4,4,32,512]{3,2,1,0:T(8,128)(2,1)}, u32[]{:S(2)}, u32[]{:S(2)}) async-start(bf16[4,4,32,512]{3,2,1,0:T(8,128)(2,1)} %pick.1), calls=%async_computation.1 | async-start | bytes 1048576 | tf_op jit(solution)/shard_map/all_to_all | solution.py:271
  28.7 0.0 collective-permute-done.refs_12_.refs_0_
  28.7 1.3 %collective-permute-start.4 = (bf16[2,2,512,256]{3,2,1,0:T(8,128)(2,1)S(1)}, bf16[2,2,512,256]{3,2,1,0:T(8,128)(2,1)}, u32[]{:S(2)}, u32[]{:S(2)}) collective-permute-start(bf16[2,2,512,256]{3,2,1,0:T(8,128)(2,1)S(1)} %collective-permute-done.refs_12_.refs_0_), channel_id=1, source_target_pairs={{1,0},{2,3},{5,4},{6,7},{9,8},{10,11},{13,12},{14,15},{17,16},{18,... | collective-permute-start | bytes 3145736 | tf_op jit(solution)/shard_map/ppermute | solution.py:26
  30.0 4.4 %collective-permute-done.1.refs_9_ = bf16[2,2,512,256]{3,2,1,0:T(8,128)(2,1)S(1)} collective-permute-done((bf16[2,2,512,256]{3,2,1,0:T(8,128)(2,1)}, bf16[2,2,512,256]{3,2,1,0:T(8,128)(2,1)S(1)}, u32[]{:S(2)}, u32[]{:S(2)}) %collective-permute-start.1) | collective-permute-done | bytes 1048608 | tf_op jit(solution)/shard_map/ppermute | solution.py:26
  34.4 1.1 %slice_bitcast_fusion = (bf16[2,512,256]{2,1,0:T(8,128)(2,1)}, bf16[2,512,256]{2,1,0:T(8,128)(2,1)}) fusion(bf16[2,2,512,256]{3,2,1,0:T(8,128)(2,1)S(1)} %collective-permute-done.1.refs_9_), kind=kLoop, calls=%fused_computation | loop fusion | bytes 2097152 | tf_op jit(solution)/shard_map/squeeze | solution.py:276
  35.4 14.0 %all-to-all-done.1.picked_ref = bf16[4,4,32,512]{3,2,1,0:T(8,128)(2,1)} async-done(((bf16[4,4,32,512]{3,2,1,0:T(8,128)(2,1)}), bf16[4,4,32,512]{3,2,1,0:T(8,128)(2,1)}, u32[]{:S(2)}, u32[]{:S(2)}) %all-to-all-start.1) | async-done | bytes 524320 | tf_op jit(solution)/shard_map/all_to_all | solution.py:271
  49.5 1.5 %collective-permute-start.2 = (bf16[2,512,256]{2,1,0:T(8,128)(2,1)}, bf16[2,512,256]{2,1,0:T(8,128)(2,1)}, u32[]{:S(2)}, u32[]{:S(2)}) collective-permute-start(bf16[2,512,256]{2,1,0:T(8,128)(2,1)} %get-tuple-element.13), channel_id=1, source_target_pairs={{2,1},{1,2},{6,5},{5,6},{10,9},{9,10},{14,13},{13,14},{18,17},{17,... | collective-permute-start | bytes 1572872 | tf_op jit(solution)/shard_map/ppermute | solution.py:26
  50.9 2.0 %turn.1.refs_0_ = bf16[512,512]{1,0:T(8,128)(2,1)} custom-call(bf16[4,4,32,512]{3,2,1,0:T(8,128)(2,1)} %all-to-all-done.1.picked_ref), custom_call_target="tpu_custom_call" | custom-call | tf_op jit(solution)/shard_map/turn/pallas_call | solution.py:284
  53.0 2.6 %collective-permute-start.12 = (bf16[512,512]{1,0:T(8,128)(2,1)}, bf16[512,512]{1,0:T(8,128)(2,1)S(1)}, u32[]{:S(2)}, u32[]{:S(2)}) collective-permute-start(bf16[512,512]{1,0:T(8,128)(2,1)} %turn.1.refs_0_), channel_id=1, source_target_pairs={{24,0},{28,4},{16,8},{20,12},{8,16},{12,20},{0,24},{4,28},{25,1},{... | collective-permute-start | bytes 1572872 | tf_op jit(solution)/shard_map/ppermute | solution.py:26
  55.5 0.6 collective-permute-start.10
  56.1 0.4 collective-permute-start.8
  56.5 0.0 collective-permute-done.2.refs_10_
  56.5 0.7 collective-permute-start.3
  57.2 11.5 %collective-permute-done.4.refs_11_ = bf16[2,2,512,256]{3,2,1,0:T(8,128)(2,1)} collective-permute-done((bf16[2,2,512,256]{3,2,1,0:T(8,128)(2,1)S(1)}, bf16[2,2,512,256]{3,2,1,0:T(8,128)(2,1)}, u32[]{:S(2)}, u32[]{:S(2)}) %collective-permute-start.4) | collective-permute-done | bytes 1048608 | tf_op jit(solution)/shard_map/ppermute | solution.py:26
  68.6 1.3 %collective-permute-start.5 = (bf16[2,512,256]{2,1,0:T(8,128)(2,1)}, bf16[2,512,256]{2,1,0:T(8,128)(2,1)S(1)}, u32[]{:S(2)}, u32[]{:S(2)}) collective-permute-start(bf16[2,512,256]{2,1,0:T(8,128)(2,1)} %collective-permute-done.2.refs_10_), channel_id=1, source_target_pairs={{1,0},{2,3},{5,4},{6,7},{9,8},{10,11},{13,12},{14,15},{17,16},{18,... | collective-permute-start | bytes 1572872 | tf_op jit(solution)/shard_map/ppermute | solution.py:26
  69.9 0.0 collective-permute-done.12.refs_6_
  69.9 0.1 collective-permute-start.7
  70.0 8.8 %collective-permute-done.10.refs_4_ = bf16[512,512]{1,0:T(8,128)(2,1)S(1)} collective-permute-done((bf16[512,512]{1,0:T(8,128)(2,1)}, bf16[512,512]{1,0:T(8,128)(2,1)S(1)}, u32[]{:S(2)}, u32[]{:S(2)}) %collective-permute-start.10) | collective-permute-done | bytes 524320 | tf_op jit(solution)/shard_map/ppermute | solution.py:26
  78.8 0.0 collective-permute-start.13
  78.8 0.0 collective-permute-done.8.refs_2_
  78.8 0.5 collective-permute-start.11
  79.3 0.0 collective-permute-done.3.refs_14_
  79.3 0.1 collective-permute-start.9
  79.4 1.9 %collective-permute-done.5.refs_13_ = bf16[2,512,256]{2,1,0:T(8,128)(2,1)S(1)} collective-permute-done((bf16[2,512,256]{2,1,0:T(8,128)(2,1)}, bf16[2,512,256]{2,1,0:T(8,128)(2,1)S(1)}, u32[]{:S(2)}, u32[]{:S(2)}) %collective-permute-start.5) | collective-permute-done | bytes 524320 | tf_op jit(solution)/shard_map/ppermute | solution.py:26
  81.3 1.3 %collective-permute-start.6 = (bf16[2,512,256]{2,1,0:T(8,128)(2,1)S(1)}, bf16[2,512,256]{2,1,0:T(8,128)(2,1)S(1)}, u32[]{:S(2)}, u32[]{:S(2)}) collective-permute-start(bf16[2,512,256]{2,1,0:T(8,128)(2,1)S(1)} %collective-permute-done.3.refs_14_), channel_id=1, source_target_pairs={{1,0},{2,3},{5,4},{6,7},{9,8},{10,11},{13,12},{14,15},{17,16},{18,... | collective-permute-start | bytes 1572872 | tf_op jit(solution)/shard_map/ppermute | solution.py:26
  82.6 0.0 collective-permute-done.7.refs_1_
  82.6 0.0 collective-permute-done.13.refs_7_
  82.6 0.0 collective-permute-done.11.refs_5_
  82.6 0.0 collective-permute-done.9.refs_3_
  82.6 0.0 copy-done
  82.6 0.0 copy-start.1
  82.6 1.0 %copy-done.1 = bf16[512,512]{1,0:T(8,128)(2,1)S(1)} copy-done((bf16[512,512]{1,0:T(8,128)(2,1)S(1)}, bf16[512,512]{1,0:T(8,128)(2,1)}, u32[]{:S(2)}) %copy-start.1) | copy-done | bytes 524312
  83.7 6.1 %early.1 = (f32[2,512,2,512]{3,2,1,0:T(2,128)}, f32[512,512]{1,0:T(8,128)S(1)}, f32[512,512]{1,0:T(8,128)S(1)}, bf16[2,512,256]{2,1,0:T(8,128)(2,1)S(1)}) custom-call(bf16[512,512]{1,0:T(8,128)(2,1)S(1)} %copy-done.1, bf16[512,512]{1,0:T(8,128)(2,1)S(1)} %collective-permute-done.7.refs_1_, bf16[512,512]{1,0:T(8,128)(2,1)S(1)} %collective-permute-done.8.refs_2_, ...), custom_call_target="tpu_custom_call" | custom-call | flops 4000000000 | bytes 2097152 | tf_op jit(solution)/shard_map/early/pallas_call | solution.py:212
  89.8 5.7 %collective-permute-done.6.refs_1_ = bf16[2,512,256]{2,1,0:T(8,128)(2,1)S(1)} collective-permute-done((bf16[2,512,256]{2,1,0:T(8,128)(2,1)S(1)}, bf16[2,512,256]{2,1,0:T(8,128)(2,1)S(1)}, u32[]{:S(2)}, u32[]{:S(2)}) %collective-permute-start.6) | collective-permute-done | bytes 524320 | tf_op jit(solution)/shard_map/ppermute | solution.py:26
  95.5 1.9 %late.1 = f32[2,512,2,512]{3,2,1,0:T(2,128)} custom-call(bf16[2,2,512,256]{3,2,1,0:T(8,128)(2,1)S(1)} %collective-permute-done.refs_12_.refs_0_, bf16[2,512,256]{2,1,0:T(8,128)(2,1)S(1)} %collective-permute-done.6.refs_1_, f32[512,512]{1,0:T(8,128)S(1)} %get-tuple-element.17.refs_2_, ...), custom_call_target="tpu_custom_call", output_to_operand_aliasing={{}: (5, {})} | custom-call | tf_op jit(solution)/shard_map/late/pallas_call | solution.py:233
Async XLA Ops:
  0.0 20.6 %all-to-all-start = ((bf16[8,32,2048]{2,1,0:T(8,128)(2,1)}), bf16[8,32,2048]{2,1,0:T(8,128)(2,1)S(1)}, u32[]{:S(2)}, u32[]{:S(2)}) async-start(bf16[8,32,2048]{2,1,0:T(8,128)(2,1)} %bitcast.8), calls=%async_computation | async-start | bytes 2097152 | tf_op jit(solution)/shard_map/all_to_all | solution.py:260
  8.2 26.2 %collective-permute-start.1 = (bf16[2,2,512,256]{3,2,1,0:T(8,128)(2,1)}, bf16[2,2,512,256]{3,2,1,0:T(8,128)(2,1)S(1)}, u32[]{:S(2)}, u32[]{:S(2)}) collective-permute-start(bf16[2,2,512,256]{3,2,1,0:T(8,128)(2,1)} %taper.1.refs_8_), channel_id=1, source_target_pairs={{1,0},{0,1},{3,2},{2,3},{5,4},{4,5},{7,6},{6,7},{9,8},{8,9},{11,10... | collective-permute-start | bytes 3145736 | tf_op jit(solution)/shard_map/ppermute | solution.py:26
  9.8 18.9 %collective-permute-start = (bf16[2,2,512,256]{3,2,1,0:T(8,128)(2,1)}, bf16[2,2,512,256]{3,2,1,0:T(8,128)(2,1)S(1)}, u32[]{:S(2)}, u32[]{:S(2)}) collective-permute-start(bf16[2,2,512,256]{3,2,1,0:T(8,128)(2,1)} %taper.1.refs_8_), channel_id=1, source_target_pairs={{2,1},{1,2},{6,5},{5,6},{10,9},{9,10},{14,13},{13,14},{18,17},{17,... | collective-permute-start | bytes 3145736 | tf_op jit(solution)/shard_map/ppermute | solution.py:26
  20.6 1.0 %copy-start.2 = (bf16[8,32,2048]{2,1,0:T(8,128)(2,1)}, bf16[8,32,2048]{2,1,0:T(8,128)(2,1)S(1)}, u32[]{:S(2)}) copy-start(bf16[8,32,2048]{2,1,0:T(8,128)(2,1)S(1)} %all-to-all-done.shares_ref) | copy-start | bytes 3145732
  23.7 58.9 %copy-start = (bf16[2,2,512,256]{3,2,1,0:T(8,128)(2,1)S(1)}, bf16[2,2,512,256]{3,2,1,0:T(8,128)(2,1)}, u32[]{:S(2)}) copy-start(bf16[2,2,512,256]{3,2,1,0:T(8,128)(2,1)} %taper.1.refs_8_) | copy-start | bytes 3145732
  23.7 25.8 %all-to-all-start.1 = ((bf16[4,4,32,512]{3,2,1,0:T(8,128)(2,1)}), bf16[4,4,32,512]{3,2,1,0:T(8,128)(2,1)}, u32[]{:S(2)}, u32[]{:S(2)}) async-start(bf16[4,4,32,512]{3,2,1,0:T(8,128)(2,1)} %pick.1), calls=%async_computation.1 | async-start | bytes 1048576 | tf_op jit(solution)/shard_map/all_to_all | solution.py:271
  28.7 39.9 %collective-permute-start.4 = (bf16[2,2,512,256]{3,2,1,0:T(8,128)(2,1)S(1)}, bf16[2,2,512,256]{3,2,1,0:T(8,128)(2,1)}, u32[]{:S(2)}, u32[]{:S(2)}) collective-permute-start(bf16[2,2,512,256]{3,2,1,0:T(8,128)(2,1)S(1)} %collective-permute-done.refs_12_.refs_0_), channel_id=1, source_target_pairs={{1,0},{2,3},{5,4},{6,7},{9,8},{10,11},{13,12},{14,15},{17,16},{18,... | collective-permute-start | bytes 3145736 | tf_op jit(solution)/shard_map/ppermute | solution.py:26
  49.5 7.0 %collective-permute-start.2 = (bf16[2,512,256]{2,1,0:T(8,128)(2,1)}, bf16[2,512,256]{2,1,0:T(8,128)(2,1)}, u32[]{:S(2)}, u32[]{:S(2)}) collective-permute-start(bf16[2,512,256]{2,1,0:T(8,128)(2,1)} %get-tuple-element.13), channel_id=1, source_target_pairs={{2,1},{1,2},{6,5},{5,6},{10,9},{9,10},{14,13},{13,14},{18,17},{17,... | collective-permute-start | bytes 1572872 | tf_op jit(solution)/shard_map/ppermute | solution.py:26
  53.0 16.9 %collective-permute-start.12 = (bf16[512,512]{1,0:T(8,128)(2,1)}, bf16[512,512]{1,0:T(8,128)(2,1)S(1)}, u32[]{:S(2)}, u32[]{:S(2)}) collective-permute-start(bf16[512,512]{1,0:T(8,128)(2,1)} %turn.1.refs_0_), channel_id=1, source_target_pairs={{24,0},{28,4},{16,8},{20,12},{8,16},{12,20},{0,24},{4,28},{25,1},{... | collective-permute-start | bytes 1572872 | tf_op jit(solution)/shard_map/ppermute | solution.py:26
  55.5 23.3 %collective-permute-start.10 = (bf16[512,512]{1,0:T(8,128)(2,1)}, bf16[512,512]{1,0:T(8,128)(2,1)S(1)}, u32[]{:S(2)}, u32[]{:S(2)}) collective-permute-start(bf16[512,512]{1,0:T(8,128)(2,1)} %turn.1.refs_0_), channel_id=1, source_target_pairs={{16,0},{20,4},{24,8},{28,12},{0,16},{4,20},{8,24},{12,28},{17,1},{... | collective-permute-start | bytes 1572872 | tf_op jit(solution)/shard_map/ppermute | solution.py:26
  56.1 22.7 %collective-permute-start.8 = (bf16[512,512]{1,0:T(8,128)(2,1)}, bf16[512,512]{1,0:T(8,128)(2,1)S(1)}, u32[]{:S(2)}, u32[]{:S(2)}) collective-permute-start(bf16[512,512]{1,0:T(8,128)(2,1)} %turn.1.refs_0_), channel_id=1, source_target_pairs={{8,0},{12,4},{0,8},{4,12},{24,16},{28,20},{16,24},{20,28},{9,1},{1... | collective-permute-start | bytes 1572872 | tf_op jit(solution)/shard_map/ppermute | solution.py:26
  56.5 22.9 %collective-permute-start.3 = (bf16[2,512,256]{2,1,0:T(8,128)(2,1)}, bf16[2,512,256]{2,1,0:T(8,128)(2,1)S(1)}, u32[]{:S(2)}, u32[]{:S(2)}) collective-permute-start(bf16[2,512,256]{2,1,0:T(8,128)(2,1)} %get-tuple-element.14), channel_id=1, source_target_pairs={{2,1},{1,2},{6,5},{5,6},{10,9},{9,10},{14,13},{13,14},{18,17},{17,... | collective-permute-start | bytes 1572872 | tf_op jit(solution)/shard_map/ppermute | solution.py:26
  68.6 12.7 %collective-permute-start.5 = (bf16[2,512,256]{2,1,0:T(8,128)(2,1)}, bf16[2,512,256]{2,1,0:T(8,128)(2,1)S(1)}, u32[]{:S(2)}, u32[]{:S(2)}) collective-permute-start(bf16[2,512,256]{2,1,0:T(8,128)(2,1)} %collective-permute-done.2.refs_10_), channel_id=1, source_target_pairs={{1,0},{2,3},{5,4},{6,7},{9,8},{10,11},{13,12},{14,15},{17,16},{18,... | collective-permute-start | bytes 1572872 | tf_op jit(solution)/shard_map/ppermute | solution.py:26
  69.9 12.6 %collective-permute-start.7 = (bf16[512,512]{1,0:T(8,128)(2,1)}, bf16[512,512]{1,0:T(8,128)(2,1)S(1)}, u32[]{:S(2)}, u32[]{:S(2)}) collective-permute-start(bf16[512,512]{1,0:T(8,128)(2,1)} %turn.1.refs_0_), channel_id=1, source_target_pairs={{4,0},{0,4},{12,8},{8,12},{20,16},{16,20},{28,24},{24,28},{5,1},{1... | collective-permute-start | bytes 1572872 | tf_op jit(solution)/shard_map/ppermute | solution.py:26
  78.8 3.8 %collective-permute-start.13 = (bf16[512,512]{1,0:T(8,128)(2,1)S(1)}, bf16[512,512]{1,0:T(8,128)(2,1)S(1)}, u32[]{:S(2)}, u32[]{:S(2)}) collective-permute-start(bf16[512,512]{1,0:T(8,128)(2,1)S(1)} %collective-permute-done.12.refs_6_), channel_id=1, source_target_pairs={{4,0},{0,4},{12,8},{8,12},{20,16},{16,20},{28,24},{24,28},{5,1},{1... | collective-permute-start | bytes 1572872 | tf_op jit(solution)/shard_map/ppermute | solution.py:26
  78.8 3.8 %collective-permute-start.11 = (bf16[512,512]{1,0:T(8,128)(2,1)S(1)}, bf16[512,512]{1,0:T(8,128)(2,1)S(1)}, u32[]{:S(2)}, u32[]{:S(2)}) collective-permute-start(bf16[512,512]{1,0:T(8,128)(2,1)S(1)} %collective-permute-done.10.refs_4_), channel_id=1, source_target_pairs={{4,0},{0,4},{12,8},{8,12},{20,16},{16,20},{28,24},{24,28},{5,1},{1... | collective-permute-start | bytes 1572872 | tf_op jit(solution)/shard_map/ppermute | solution.py:26
  79.3 3.3 %collective-permute-start.9 = (bf16[512,512]{1,0:T(8,128)(2,1)S(1)}, bf16[512,512]{1,0:T(8,128)(2,1)S(1)}, u32[]{:S(2)}, u32[]{:S(2)}) collective-permute-start(bf16[512,512]{1,0:T(8,128)(2,1)S(1)} %collective-permute-done.8.refs_2_), channel_id=1, source_target_pairs={{4,0},{0,4},{12,8},{8,12},{20,16},{16,20},{28,24},{24,28},{5,1},{1... | collective-permute-start | bytes 1572872 | tf_op jit(solution)/shard_map/ppermute | solution.py:26
  81.3 14.3 %collective-permute-start.6 = (bf16[2,512,256]{2,1,0:T(8,128)(2,1)S(1)}, bf16[2,512,256]{2,1,0:T(8,128)(2,1)S(1)}, u32[]{:S(2)}, u32[]{:S(2)}) collective-permute-start(bf16[2,512,256]{2,1,0:T(8,128)(2,1)S(1)} %collective-permute-done.3.refs_14_), channel_id=1, source_target_pairs={{1,0},{2,3},{5,4},{6,7},{9,8},{10,11},{13,12},{14,15},{17,16},{18,... | collective-permute-start | bytes 1572872 | tf_op jit(solution)/shard_map/ppermute | solution.py:26
  82.6 1.0 %copy-start.1 = (bf16[512,512]{1,0:T(8,128)(2,1)S(1)}, bf16[512,512]{1,0:T(8,128)(2,1)}, u32[]{:S(2)}) copy-start(bf16[512,512]{1,0:T(8,128)(2,1)} %turn.1.refs_0_) | copy-start | bytes 1572868

commit v4 on v1

v4 whole, which is shorter than its diff:
```python
import functools

import jax
import jax.numpy as jnp
from jax import lax
from jax.experimental import pallas as pl
from jax.experimental.pallas import tpu as pltpu
from jax.sharding import PartitionSpec as P

BLOCKS = 4
EDGE = 64
LANES = 128
LABEL_ROWS = 16
PICK_FLOPS = 0 * 10**9
TAPER_FLOPS = 10**9
SUM_FLOPS = 4 * 10**9
LAST_FLOPS = 10**9
ROWS_BY_ROWS = (((1,), (1,)), ((), ()))
WHOLE = pl.BlockSpec(memory_space=pltpu.VMEM)
SCALARS = pl.BlockSpec(memory_space=pltpu.SMEM)
IN_PLACE = pl.BlockSpec(memory_space=pl.ANY)


def exchange(value, axis, distance, among=None):
    pairs = [(i ^ distance, i) for i in range(lax.axis_size(axis))]
    return lax.ppermute(value, axis, [p for p in pairs if among is None or p in among])


def after(value, *earlier):
    return lax.optimization_barrier((value, earlier))[0]


def settings(flops, megabytes=40):
    return {
        "cost_estimate": pl.CostEstimate(flops=flops, bytes_accessed=2**21, transcendentals=0),
        "compiler_params": pltpu.CompilerParams(vmem_limit_bytes=megabytes * 2**20),
    }


def unit_bin(unit):
    return lax.bitwise_xor(lax.axis_index("rbin"), unit)


def minus_weight(unit, gain_ref, start_ref, end_ref, bins_ref):
    shots, points = start_ref.shape[1], bins_ref.shape[1]
    labels = bins_ref[pl.ds(unit_bin(unit), 1), :].astype(jnp.int32)
    column = unit_bin(unit) * points + lax.broadcasted_iota(jnp.int32, labels.shape, 1)
    gain = jnp.zeros(labels.shape, jnp.float32)
    for label in range(gain_ref.shape[0]):
        gain = gain + jnp.where(labels == label, gain_ref[label], 0.0)
    start = jnp.broadcast_to(start_ref[...], (LANES, shots)).T[:, :1]
    end = jnp.broadcast_to(end_ref[...], (LANES, shots)).T[:, :1]
    distance = jnp.minimum(column - start, end - 1 - column)
    ramped = jnp.minimum((distance + 1).astype(jnp.float32) / EDGE, 1.0)
    return jnp.where(distance >= 0, ramped, 0.0) * -gain


def tapered(values, weight):
    return (values.astype(jnp.float32) * weight).astype(jnp.bfloat16)


def taper_kernel(units, gain_ref, start_ref, end_ref, bins_ref, *refs):
    for unit, raw_ref, out_ref in zip(units, refs[: len(units)], refs[len(units) :]):
        weight = minus_weight(unit, gain_ref, start_ref, end_ref, bins_ref)
        for freq in range(raw_ref.shape[0]):
            for part in range(2):
                out_ref[freq, part] = tapered(raw_ref[freq, part], weight)


def taper(units, raw, taper_args):
    return pl.pallas_call(
        functools.partial(taper_kernel, units),
        in_specs=[SCALARS] + [WHOLE] * (3 + len(raw)),
        out_specs=[WHOLE] * len(raw),
        out_shape=[jax.ShapeDtypeStruct(r.shape, r.dtype) for r in raw],
        name="taper",
        **settings(TAPER_FLOPS, 16),
    )(*taper_args, *raw)


def share_kernel(bins, recorded_ref, shares_ref):
    _, freqs, _, _, receivers = recorded_ref.shape
    parts = shares_ref.shape[0] // (2 * freqs)
    own = receivers // bins
    part = own // parts
    for slot in range(shares_ref.shape[0]):
        for unit in range(bins):
            first = unit * own + slot % parts * part
            shares_ref[slot, :, unit * part : (unit + 1) * part] = recorded_ref[
                0, slot // parts // 2, slot // parts % 2, :, first : first + part
            ]


def pick_kernel(owner_ref, bin_ref, shares_ref, picked_ref):
    bins, points, part = picked_ref.shape
    points -= LABEL_ROWS
    rows = points // BLOCKS
    labels = jnp.broadcast_to(bin_ref[...].astype(jnp.float32), (LABEL_ROWS, part))
    for unit in range(bins):
        span = slice(unit * part, (unit + 1) * part)
        for block in range(BLOCKS):
            here = slice(block * rows, (block + 1) * rows)
            picked_ref[unit, here] = shares_ref[owner_ref[block], :, span]
        picked_ref[unit, points:] = labels.astype(jnp.bfloat16)


def wanted_shares(recorded, block_owner, taper_bin, bins):
    _, freqs, _, rows, receivers = recorded.shape
    slots = lax.axis_size("shot")
    parts = slots // (2 * freqs)
    part = receivers // bins // parts
    points = BLOCKS * rows
    if part != points:
        shares = recorded.reshape(freqs, 2, rows, bins, parts, part)
        shares = shares.transpose(0, 1, 4, 3, 2, 5).reshape(slots, bins, rows, part)
        shares = lax.all_to_all(shares, "shot", 0, 0)
        picked = shares[block_owner].transpose(1, 0, 2, 3).reshape(bins, points, part)
        picked = lax.all_to_all(picked, "rbin", 0, 0)
        labels = lax.all_gather(taper_bin, "rbin").astype(jnp.float32)
        return turn(picked, points)[0], labels
    shares = pl.pallas_call(
        functools.partial(share_kernel, bins),
        in_specs=[WHOLE],
        out_specs=WHOLE,
        out_shape=jax.ShapeDtypeStruct((slots, rows, bins * part), recorded.dtype),
        name="share",
        **settings(0, 8),
    )(recorded)
    shares = lax.all_to_all(shares, "shot", 0, 0)
    picked = pl.pallas_call(
        pick_kernel,
        in_specs=[SCALARS, WHOLE, WHOLE],
        out_specs=WHOLE,
        out_shape=jax.ShapeDtypeStruct((bins, points + LABEL_ROWS, part), recorded.dtype),
        name="pick",
        **settings(PICK_FLOPS, 8),
    )(block_owner, taper_bin.reshape(1, points), shares)
    return turn(lax.all_to_all(picked, "rbin", 0, 0), points)


def turn_kernel(picked_ref, out_ref, labels_ref):
    bins, points = labels_ref.shape
    for unit in range(bins):
        values = picked_ref[unit_bin(unit), :points]
        out_ref[:, unit * points : (unit + 1) * points] = values.T
        if picked_ref.shape[1] > points:
            labels_ref[unit : unit + 1] = picked_ref[unit, points:][:1].astype(jnp.float32)


def turn(picked, points):
    bins, _, part = picked.shape
    return pl.pallas_call(
        turn_kernel,
        in_specs=[WHOLE],
        out_specs=[WHOLE, WHOLE],
        out_shape=[
            jax.ShapeDtypeStruct((part, bins * points), jnp.bfloat16),
            jax.ShapeDtypeStruct((bins, points), jnp.float32),
        ],
        name="turn",
        **settings(0, 8),
    )(picked)


def unit_product(r0, r1, g):
    def dot(a, b):
        return lax.dot_general(a, b, ROWS_BY_ROWS, preferred_element_type=jnp.float32)

    return dot(r0, g[0]) + dot(-r1, g[1]), dot(r0, g[1]) + dot(r1, g[0])


def choose(bins, freq, refs):
    values = [ref[freq] if len(ref.shape) == 4 else ref[...] for ref in refs]
    if len(values) == 1:
        return values[0]
    rbin = lax.axis_index("rbin")
    inner = jnp.logical_and(rbin > 0, rbin < bins - 1)
    return jnp.where(inner, values[0], values[1])


def sum_kernel(freqs, order, raw_units, n_operands, splits, *refs):
    refs = list(refs)
    piece_refs = [[refs.pop(0) for _ in range(n)] for n in splits]
    taper_refs = [refs.pop(0) for _ in range(4)]
    operands = [refs.pop(0) for _ in range(n_operands)]
    sums = [[refs.pop(0) for _ in range(3)] for _ in range(freqs)]
    weight_ref, held, ready, sems = refs
    shot = lax.axis_index("shot")
    copies = []
    for d, blocks in enumerate(piece_refs):
        for i, ref in enumerate(blocks):
            here = pl.ds(i * ref.shape[0], ref.shape[0])
            target = held.at[lax.bitwise_xor(shot, d), here]
            copies.append(pltpu.make_async_copy(ref, target, sems.at[d, i]))
    for copy in copies:
        copy.start()
    bins = len(order[0]) + 1
    points = weight_ref.shape[1]
    parts = len(splits) // (2 * freqs)
    part = held.shape[1]
    weight_ref[...] = minus_weight(bins - 1, *taper_refs)
    for at, unit in enumerate(raw_units):
        weight = minus_weight(unit, *taper_refs)
        for freq in range(freqs):
            values = choose(bins, freq, [operands[i] for i in order[freq][unit]])
            for c in range(2):
                ready[at, freq, c] = tapered(values[c], weight)
    for copy in copies:
        copy.wait()
    for freq in range(freqs):
        real_ref, imag_ref, left_ref = sums[freq]
        for h in range(parts):
            here = slice(h * part, (h + 1) * part)
            first = freq * 2 * parts + h
            real = imag = None
            for unit, candidates in enumerate(order[freq]):
                if unit in raw_units:
                    g = ready[raw_units.index(unit), freq]
                else:
                    g = choose(bins, freq, [operands[i] for i in candidates])
                span = slice(unit * points, (unit + 1) * points)
                a, b = unit_product(held[first, :, span], held[first + parts, :, span], g)
                real = a if real is None else real + a
                imag = b if imag is None else imag + b
            real_ref[here] = real
            imag_ref[here] = imag
            span = slice((bins - 1) * points, bins * points)
            for c in range(2):
                left_ref[c, here] = held[first + c * parts, :, span]


def last_kernel(bins, freq, n_candidates, *refs):
    candidates = refs[:n_candidates]
    real_ref, imag_ref, left_ref, weight_ref = refs[n_candidates : n_candidates + 4]
    out_ref, done, sems = refs[-3:]
    values = choose(bins, freq, candidates)
    g = [tapered(values[c], weight_ref[...]) for c in range(2)]
    chunks = sems.shape[0]
    rows = real_ref.shape[0] // chunks
    leaving = []
    for chunk in range(chunks):
        here = slice(chunk * rows, (chunk + 1) * rows)
        a, b = unit_product(left_ref[0, here], left_ref[1, here], g)
        done[here, 0, :] = real_ref[here] + a
        done[here, 1, :] = imag_ref[here] + b
        leaving.append(
            pltpu.make_async_copy(done.at[here], out_ref.at[freq, here], sems.at[chunk])
        )
        leaving[-1].start()
    for copy in leaving:
        copy.wait()


def product(pieces, gathers, raw_units, taper_args):
    freqs, bins = len(gathers), len(gathers[0])
    shots, points = gathers[0][0][0].shape[-2:]
    splits = [len(blocks) for blocks in pieces]
    blocks = [block for blocks in pieces for block in blocks]
    part = pieces[0][0].shape[0]
    own = part * len(pieces) // (2 * freqs)
    operands, order = [], []
    for of_freq in gathers:
        order.append([])
        for unit in of_freq[:-1]:
            for value in unit:
                if not any(value is known for known in operands):
                    operands.append(value)
            order[-1].append([[value is o for o in operands].index(True) for value in unit])
    sum_type = jax.ShapeDtypeStruct((own, shots), jnp.float32)
    left_type = jax.ShapeDtypeStruct((2, own, points), jnp.bfloat16)
    *sums, weight = pl.pallas_call(
        functools.partial(sum_kernel, freqs, order, raw_units, len(operands), splits),
        in_specs=[IN_PLACE] * len(blocks) + [SCALARS] + [WHOLE] * (3 + len(operands)),
        out_specs=[WHOLE] * (3 * freqs + 1),
        out_shape=[sum_type, sum_type, left_type] * freqs
        + [jax.ShapeDtypeStruct((shots, points), jnp.float32)],
        scratch_shapes=[
            pltpu.VMEM((len(pieces), part, bins * points), jnp.bfloat16),
            pltpu.VMEM((max(1, len(raw_units)), freqs, 2, shots, points), jnp.bfloat16),
            pltpu.SemaphoreType.DMA((len(pieces), max(splits))),
        ],
        name="sum",
        **settings(SUM_FLOPS),
    )(*blocks, *taper_args, *operands)
    chunks = 2
    out = []
    for freq in range(freqs):
        candidates = gathers[freq][-1]
        n = len(candidates)
        out = pl.pallas_call(
            functools.partial(last_kernel, bins, freq, n),
            in_specs=[WHOLE] * (n + 4) + [IN_PLACE] * len(out),
            out_specs=[IN_PLACE],
            out_shape=[jax.ShapeDtypeStruct((freqs, own, 2, shots), jnp.float32)],
            scratch_shapes=[
                pltpu.VMEM((own, 2, shots), jnp.float32),
                pltpu.SemaphoreType.DMA((chunks,)),
            ],
            input_output_aliases={n + 4: 0} if out else {},
            name="last",
            **settings(LAST_FLOPS, 16),
        )(*candidates, *sums[3 * freq : 3 * freq + 3], weight, *out)
    return out[0]


def per_device(
    local_gathers, recorded_shots, block_owner, aperture_start, aperture_end, taper_bin, taper_gain
):
    freqs, _, shots, points = local_gathers.shape
    slots = lax.axis_size("shot")
    bins = lax.axis_size("rbin")

    piece, labels = wanted_shares(recorded_shots, block_owner, taper_bin, bins)
    taper_args = (
        taper_gain,
        aperture_start.reshape(1, shots),
        aperture_end.reshape(1, shots),
        labels,
    )

    if bins == 4:
        inner, outward = [(1, 2), (2, 1)], [(1, 0), (2, 3)]
        near = exchange(local_gathers, "rbin", 1)
        across = exchange(local_gathers, "rbin", 3, inner)
        second = exchange(across, "rbin", 1, outward)
        units = taper([0, 1], [local_gathers, near], taper_args)
        over, down, corner = [exchange(piece, "shot", d) for d in (2, 4, 6)]
        beside = exchange(piece, "shot", 1)
        first = exchange(after(near[0], across), "rbin", 3, inner)
        near_1 = after(near[1], first)
        first_g, second, units = lax.optimization_barrier((first, second, units))
        passed_0 = exchange(first_g, "rbin", 1, outward)
        other = exchange(near_1, "rbin", 3, inner)
        over, down, corner = lax.optimization_barrier((over, down, corner))
        passed_1 = exchange(other, "rbin", 1, outward)
        pieces = [[piece], [beside]]
        for value in (over, down, corner):
            pieces += [[value], [exchange(value, "shot", 1)]]
        gathers = [
            [[units[0]], [units[1]], [first, second], [across, passed_0]],
            [[units[0]], [units[1]], [other, second], [across, passed_1]],
        ]
        pieces[0] = [after(piece, passed_0)]
        return product(pieces, gathers, [2], taper_args)
    else:
        raw = [local_gathers] + [exchange(local_gathers, "rbin", d) for d in range(1, bins)]
        units = [taper([d], [raw[d]], taper_args)[0] for d in range(bins - 1)] + [raw[-1]]
        gathers = [[[unit] for unit in units]] * freqs
        raw_units = []

    if slots == 8:
        half = piece.shape[0] // 2
        over = exchange(piece, "shot", 2)
        down = exchange(piece, "shot", 4)
        corner = [exchange(over[:half], "shot", 4), exchange(down[half:], "shot", 2)]
        pieces = {0: [piece], 2: [over], 4: [down], 6: corner}
    else:
        pieces = {d: [exchange(piece, "shot", d) if d else piece] for d in range(0, slots, 2)}
    for d in range(0, slots, 2):
        pieces[d + 1] = [exchange(p, "shot", 1) for p in pieces[d]]
    pieces = [pieces[d] for d in range(slots)]
    return product(pieces, gathers, raw_units, taper_args)


def solution(mesh):
    in_specs = (
        P(None, None, "shot", "rbin"),
        P("shot", None, None, "rbin", None),
        P(),
        P("shot"),
        P("shot"),
        P("rbin"),
        P(),
    )
    out_specs = P(None, "rbin", None, "shot")
    return jax.shard_map(
        per_device, mesh=mesh, in_specs=in_specs, out_specs=out_specs, check_vma=False
    )
```

time: 173 us -> 95.6 us (0.55)
  waiting for transfers between devices: 75.8 us -> 39.4 us
  local copies, waits for them, and re-layouts: 29.5 us -> 3.5 us
  blocking collectives: 33.3 us -> 19 us
  starting transfers between devices: 5.21 us -> 19.4 us
  Pallas kernels: 0 us -> 13.5 us
  between operations: 13.5 us -> 0.23 us
  matrix products: 9.24 us -> 0 us
  other arithmetic: 5.63 us -> 0 us
    all_gather x2 -> x0, waiting for transfers between devices: 60.4 us -> none  [the longest x1 37.9 us: per_device(): gathers = lax.all_gather(tapered, 'rbin')]
    ppermute x0 -> x14, waiting for transfers between devices: none -> 26.6 us  [exchange(): lax.ppermute(value, axis, [p for p in pairs if among is None or p in among])]
    ppermute x0 -> x14, starting transfers between devices: none -> 15.9 us  [exchange(): lax.ppermute(value, axis, [p for p in pairs if among is None or p in among])]
    all_to_all x1, blocking collectives: 33.3 us -> 19 us  [wanted_shares(): shares = lax.all_to_all(shares, 'shot', 0, 0)]
    all_gather x2 -> x0, local copies, waits for them, and re-layouts: 13.8 us -> none  [the longest x1 7.44 us: per_device(): gathers = lax.all_gather(tapered, 'rbin')]
    pallas_call x0 -> x7, Pallas kernels: none -> 13.5 us  [the longest x1 6.22 us: product(): pl.pallas_call(functools.partial(sum_kernel, freqs, order, raw_units, len...]
    dot_general x4 -> x0, matrix products: 9.24 us -> none  [dot(): lax.dot_general(a, b, (((2,), (2,)), ((0,), (0,))), preferred_element_typ...]
    reshape x1 -> x0, local copies, waits for them, and re-layouts: 7.78 us -> none  [per_device(): g = gathers.transpose(1, 2, 3, 0, 4).reshape(freqs, 2, shots, bins * points)]
  transfers between devices with their start and end apart: 3 -> 15, of which waited for: 3 -> 6; matrix products, arithmetic and copies ran while one was open for 10% -> 1% of each run, Pallas kernels for 0% -> 12%
where the time goes in v4:
time: 95.6 us; the launch traced here: 95.1 us
  waiting for transfers between devices  39.4 us (41%)
  starting transfers between devices  19.4 us (20%)
  blocking collectives  19 us (20%)
  Pallas kernels  13.5 us (14%)
  local copies, waits for them, and re-layouts  3.5 us (4%)
    ppermute x14, waiting for transfers between devices, exchange(): lax.ppermute(value, axis, [p for p in pairs if among is None or p in among])  26.6 us
    all_to_all x1, blocking collectives, wanted_shares(): shares = lax.all_to_all(shares, 'shot', 0, 0)  19 us
    ppermute x14, starting transfers between devices, exchange(): lax.ppermute(value, axis, [p for p in pairs if among is None or p in among])  15.9 us
    all_to_all x1, waiting for transfers between devices, wanted_shares(): return turn(lax.all_to_all(picked, 'rbin', 0, 0), points)  12.8 us
    pallas_call x1, Pallas kernels, product(): pl.pallas_call(functools.partial(sum_kernel, freqs, order, raw_units, len...  6.22 us
    pallas_call x2, Pallas kernels, product(): pl.pallas_call(functools.partial(last_kernel, bins, freq, n), in_specs=[W...  3.95 us
    all_to_all x1, starting transfers between devices, wanted_shares(): return turn(lax.all_to_all(picked, 'rbin', 0, 0), points)  3.47 us
    unnamed x14, local copies, waits for them, and re-layouts  2.47 us
  transfers between devices with their start and end apart: 15, of which 6 were waited for; matrix products, arithmetic and copies ran while one was open for 1% of the time, Pallas kernels for 12%

profile of v4, /device:TPU:0, one launch (start us, length us, event | category | flops | bytes accessed | tf_op | source)
XLA Modules:
  0.0 95.1 jit_solution(6958773185769241016)
XLA Ops:
  0.0 0.7 collective-permute-start
  0.7 5.8 %collective-permute-start.1 = (bf16[2,2,512,256]{3,2,1,0:T(8,128)(2,1)}, bf16[2,2,512,256]{3,2,1,0:T(8,128)(2,1)S(1)}, u32[]{:S(2)}, u32[]{:S(2)}) collective-permute-start(bf16[2,2,512,256]{3,2,1,0:T(8,128)(2,1)} %refs_0_.1), channel_id=1, source_target_pairs={{1,0},{0,1},{3,2},{2,3},{5,4},{4,5},{7,6},{6,7},{9,8},{8,9},{11,10... | collective-permute-start | bytes 3145736 | tf_op jit(solution)/shard_map/ppermute | solution.py:26
  6.6 1.2 %copy-done = bf16[1,2,2,64,2048]{4,3,2,1,0:T(8,128)(2,1)S(1)} copy-done((bf16[1,2,2,64,2048]{4,3,2,1,0:T(8,128)(2,1)S(1)}, bf16[1,2,2,64,2048]{4,3,2,1,0:T(8,128)(2,1)}, u32[]{:S(2)}) %copy-start) | copy-done | bytes 1048600
  7.8 0.1 share.1
  7.9 0.0 copy-start.4
  7.9 0.0 copy-start.5
  7.9 0.0 copy-start.6
  7.9 19.0 %all_to_all.10.shares_ref = bf16[8,64,1024]{2,1,0:T(8,128)(2,1)S(1)} all-to-all(bf16[8,64,1024]{2,1,0:T(8,128)(2,1)S(1)} %share.1), channel_id=1, replica_groups=mesh['shot'=8,'rbin'=4] {'shot'}, dimensions={0} | all-to-all | bytes 2097152 | tf_op jit(solution)/shard_map/all_to_all | solution.py:129
  26.9 0.0 copy-done.1
  26.9 0.0 copy-done.2
  26.9 1.4 %pick.1 = bf16[4,272,256]{2,1,0:T(8,128)(2,1)} custom-call(s32[4]{0:T(128)S(1)} %copy-done.2, s32[1,256]{1,0:T(1,128)S(1)} %bitcast.7, bf16[8,64,1024]{2,1,0:T(8,128)(2,1)S(1)} %all_to_all.10.shares_ref), custom_call_target="tpu_custom_call" | custom-call | bytes 2097152 | tf_op jit(solution)/shard_map/pick/pallas_call | solution.py:130
  28.3 3.5 %all-to-all-start.1 = ((bf16[4,272,256]{2,1,0:T(8,128)(2,1)}), bf16[4,272,256]{2,1,0:T(8,128)(2,1)S(1)}, u32[]{:S(2)}, u32[]{:S(2)}) async-start(bf16[4,272,256]{2,1,0:T(8,128)(2,1)} %pick.1), calls=%async_computation.1 | async-start | bytes 1114112 | tf_op jit(solution)/shard_map/all_to_all | solution.py:138
  31.8 0.0 collective-permute-done.refs_0_
  31.8 1.3 %collective-permute-start.5 = (bf16[2,2,512,256]{3,2,1,0:T(8,128)(2,1)S(1)}, bf16[2,2,512,256]{3,2,1,0:T(8,128)(2,1)}, u32[]{:S(2)}, u32[]{:S(2)}) collective-permute-start(bf16[2,2,512,256]{3,2,1,0:T(8,128)(2,1)S(1)} %collective-permute-done.refs_0_), channel_id=1, source_target_pairs={{1,0},{2,3},{5,4},{6,7},{9,8},{10,11},{13,12},{14,15},{17,16},{18,... | collective-permute-start | bytes 3145736 | tf_op jit(solution)/shard_map/ppermute | solution.py:26
  33.1 0.0 collective-permute-done.1.refs_1_
  33.1 1.0 %slice_bitcast_fusion = (bf16[2,512,256]{2,1,0:T(8,128)(2,1)}, bf16[2,512,256]{2,1,0:T(8,128)(2,1)}) fusion(bf16[2,2,512,256]{3,2,1,0:T(8,128)(2,1)S(1)} %collective-permute-done.1.refs_1_), kind=kLoop, calls=%fused_computation | loop fusion | bytes 2097152 | tf_op jit(solution)/shard_map/squeeze | solution.py:329
  34.2 0.7 collective-permute-start.2
  34.8 12.8 %all-to-all-done.1.picked_ref = bf16[4,272,256]{2,1,0:T(8,128)(2,1)S(1)} async-done(((bf16[4,272,256]{2,1,0:T(8,128)(2,1)}), bf16[4,272,256]{2,1,0:T(8,128)(2,1)S(1)}, u32[]{:S(2)}, u32[]{:S(2)}) %all-to-all-start.1) | async-done | bytes 557088 | tf_op jit(solution)/shard_map/all_to_all | solution.py:138
  47.7 0.2 turn.1
  47.9 1.2 %collective-permute-start.10 = (bf16[256,1024]{1,0:T(8,128)(2,1)S(1)}, bf16[256,1024]{1,0:T(8,128)(2,1)S(1)}, u32[]{:S(2)}, u32[]{:S(2)}) collective-permute-start(bf16[256,1024]{1,0:T(8,128)(2,1)S(1)} %get-tuple-element.33.refs_0_), channel_id=1, source_target_pairs={{24,0},{28,4},{16,8},{20,12},{8,16},{12,20},{0,24},{4,28},{25,1},{... | collective-permute-start | bytes 1572872 | tf_op jit(solution)/shard_map/ppermute | solution.py:26
  49.1 0.9 collective-permute-start.8
  50.0 1.5 %collective-permute-start.9 = (bf16[256,1024]{1,0:T(8,128)(2,1)S(1)}, bf16[256,1024]{1,0:T(8,128)(2,1)S(1)}, u32[]{:S(2)}, u32[]{:S(2)}) collective-permute-start(bf16[256,1024]{1,0:T(8,128)(2,1)S(1)} %get-tuple-element.33.refs_0_), channel_id=1, source_target_pairs={{16,0},{20,4},{24,8},{28,12},{0,16},{4,20},{8,24},{12,28},{17,1},{... | collective-permute-start | bytes 1572872 | tf_op jit(solution)/shard_map/ppermute | solution.py:26
  51.4 0.0 collective-permute-done.2.refs_14_
  51.4 0.7 collective-permute-start.3
  52.1 0.0 copy-done.4
  52.1 0.0 copy-start.3
  52.2 1.2 %copy-done.3 = bf16[2,2,512,256]{3,2,1,0:T(8,128)(2,1)S(1)} copy-done((bf16[2,2,512,256]{3,2,1,0:T(8,128)(2,1)S(1)}, bf16[2,2,512,256]{3,2,1,0:T(8,128)(2,1)}, u32[]{:S(2)}) %copy-start.3) | copy-done | bytes 1048600
  53.4 1.7 %taper.1 = (bf16[2,2,512,256]{3,2,1,0:T(8,128)(2,1)S(1)}, bf16[2,2,512,256]{3,2,1,0:T(8,128)(2,1)S(1)}) custom-call(f32[8]{0:T(128)S(1)} %copy-done.6, s32[1,512]{1,0:T(1,128)S(1)} %bitcast.8, s32[1,512]{1,0:T(1,128)S(1)} %bitcast.10, f32[4,256]{1,0:T(4,128)S(1)} %get-tuple-element.29.bins_ref.refs_11_, bf16[2,2,512,256]{3,2,1,0:T(8,128)(2,1)S(1)} %copy-done.3, ...), custom_call_target="tpu_custom_call" | custom-call | flops 1000000000 | bytes 2097152 | tf_op jit(solution)/shard_map/taper/pallas_call | solution.py:71
  55.1 10.4 %collective-permute-done.5.refs_15_ = bf16[2,2,512,256]{3,2,1,0:T(8,128)(2,1)} collective-permute-done((bf16[2,2,512,256]{3,2,1,0:T(8,128)(2,1)S(1)}, bf16[2,2,512,256]{3,2,1,0:T(8,128)(2,1)}, u32[]{:S(2)}, u32[]{:S(2)}) %collective-permute-start.5) | collective-permute-done | bytes 1048608 | tf_op jit(solution)/shard_map/ppermute | solution.py:26
  65.5 1.3 %collective-permute-start.6 = (bf16[2,512,256]{2,1,0:T(8,128)(2,1)S(1)}, bf16[2,512,256]{2,1,0:T(8,128)(2,1)S(1)}, u32[]{:S(2)}, u32[]{:S(2)}) collective-permute-start(bf16[2,512,256]{2,1,0:T(8,128)(2,1)S(1)} %collective-permute-done.2.refs_14_), channel_id=1, source_target_pairs={{1,0},{2,3},{5,4},{6,7},{9,8},{10,11},{13,12},{14,15},{17,16},{18,... | collective-permute-start | bytes 1572872 | tf_op jit(solution)/shard_map/ppermute | solution.py:26
  66.8 0.0 collective-permute-done.10.refs_6_
  66.8 0.1 collective-permute-start.7
  66.9 4.1 %collective-permute-done.8.refs_2_ = bf16[256,1024]{1,0:T(8,128)(2,1)S(1)} collective-permute-done((bf16[256,1024]{1,0:T(8,128)(2,1)S(1)}, bf16[256,1024]{1,0:T(8,128)(2,1)S(1)}, u32[]{:S(2)}, u32[]{:S(2)}) %collective-permute-start.8) | collective-permute-done | bytes 524320 | tf_op jit(solution)/shard_map/ppermute | solution.py:26
  71.0 0.9 collective-permute-done.9.refs_4_
  71.9 0.0 collective-permute-start.11
  71.9 0.5 collective-permute-start.12
  72.4 0.0 collective-permute-done.3.refs_16_
  72.4 0.0 collective-permute-start.13
  72.4 7.4 %collective-permute-done.6.refs_1_ = bf16[2,512,256]{2,1,0:T(8,128)(2,1)S(1)} collective-permute-done((bf16[2,512,256]{2,1,0:T(8,128)(2,1)S(1)}, bf16[2,512,256]{2,1,0:T(8,128)(2,1)S(1)}, u32[]{:S(2)}, u32[]{:S(2)}) %collective-permute-start.6) | collective-permute-done | bytes 524320 | tf_op jit(solution)/shard_map/ppermute | solution.py:26
  79.8 1.3 %collective-permute-start.4 = (bf16[2,512,256]{2,1,0:T(8,128)(2,1)S(1)}, bf16[2,512,256]{2,1,0:T(8,128)(2,1)S(1)}, u32[]{:S(2)}, u32[]{:S(2)}) collective-permute-start(bf16[2,512,256]{2,1,0:T(8,128)(2,1)S(1)} %collective-permute-done.3.refs_16_), channel_id=1, source_target_pairs={{1,0},{2,3},{5,4},{6,7},{9,8},{10,11},{13,12},{14,15},{17,16},{18,... | collective-permute-start | bytes 1572872 | tf_op jit(solution)/shard_map/ppermute | solution.py:26
  81.1 0.0 collective-permute-done.7.refs_1_
  81.1 0.0 collective-permute-done.11.refs_3_
  81.1 0.0 collective-permute-done.12.refs_5_
  81.1 0.0 collective-permute-done.13.refs_7_
  81.1 6.2 %sum.1 = (f32[512,512]{1,0:T(8,128)S(1)}, f32[512,512]{1,0:T(8,128)S(1)}, bf16[2,512,256]{2,1,0:T(8,128)(2,1)S(1)}, f32[512,512]{1,0:T(8,128)S(1)}, f32[512,512]...) custom-call(bf16[256,1024]{1,0:T(8,128)(2,1)S(1)} %get-tuple-element.33.refs_0_, ...), custom_call_target="tpu_custom_call" | custom-call | flops 4000000000 | bytes 2097152 | tf_op jit(solution)/shard_map/sum/pallas_call | solution.py:271
  87.4 2.0 %last.2.refs_6_ = f32[2,512,2,512]{3,2,1,0:T(2,128)} custom-call(bf16[2,2,512,256]{3,2,1,0:T(8,128)(2,1)S(1)} %collective-permute-done.refs_0_, bf16[2,512,256]{2,1,0:T(8,128)(2,1)S(1)} %collective-permute-done.6.refs_1_, f32[512,512]{1,0:T(8,128)S(1)} %get-tuple-element.44.refs_2_, f32[512,512]{1,0:T(8,128)S(1)} %get-tuple-element.45.refs_3_, ...), custom_call_target="tpu_custom_call" | custom-call | flops 1000000000 | bytes 2097152 | tf_op jit(solution)/shard_map/last/pallas_call | solution.py:290
  89.3 3.8 %collective-permute-done.4.refs_1_ = bf16[2,512,256]{2,1,0:T(8,128)(2,1)S(1)} collective-permute-done((bf16[2,512,256]{2,1,0:T(8,128)(2,1)S(1)}, bf16[2,512,256]{2,1,0:T(8,128)(2,1)S(1)}, u32[]{:S(2)}, u32[]{:S(2)}) %collective-permute-start.4) | collective-permute-done | bytes 524320 | tf_op jit(solution)/shard_map/ppermute | solution.py:26
  93.2 2.0 %last.3 = f32[2,512,2,512]{3,2,1,0:T(2,128)} custom-call(bf16[2,2,512,256]{3,2,1,0:T(8,128)(2,1)S(1)} %collective-permute-done.refs_0_, bf16[2,512,256]{2,1,0:T(8,128)(2,1)S(1)} %collective-permute-done.4.refs_1_, f32[512,512]{1,0:T(8,128)S(1)} %get-tuple-element.40.refs_2_, ...), custom_call_target="tpu_custom_call", output_to_operand_aliasing={{}: (6, {})} | custom-call | flops 1000000000 | bytes 2097152 | tf_op jit(solution)/shard_map/last/pallas_call | solution.py:290
  (5 shorter events, 0.0 us)
Async XLA Ops:
  0.0 31.8 %collective-permute-start = (bf16[2,2,512,256]{3,2,1,0:T(8,128)(2,1)}, bf16[2,2,512,256]{3,2,1,0:T(8,128)(2,1)S(1)}, u32[]{:S(2)}, u32[]{:S(2)}) collective-permute-start(bf16[2,2,512,256]{3,2,1,0:T(8,128)(2,1)} %refs_0_.1), channel_id=1, source_target_pairs={{2,1},{1,2},{6,5},{5,6},{10,9},{9,10},{14,13},{13,14},{18,17},{17,... | collective-permute-start | bytes 3145736 | tf_op jit(solution)/shard_map/ppermute | solution.py:26
  0.7 32.4 %collective-permute-start.1 = (bf16[2,2,512,256]{3,2,1,0:T(8,128)(2,1)}, bf16[2,2,512,256]{3,2,1,0:T(8,128)(2,1)S(1)}, u32[]{:S(2)}, u32[]{:S(2)}) collective-permute-start(bf16[2,2,512,256]{3,2,1,0:T(8,128)(2,1)} %refs_0_.1), channel_id=1, source_target_pairs={{1,0},{0,1},{3,2},{2,3},{5,4},{4,5},{7,6},{6,7},{9,8},{8,9},{11,10... | collective-permute-start | bytes 3145736 | tf_op jit(solution)/shard_map/ppermute | solution.py:26
  6.6 1.2 %copy-start = (bf16[1,2,2,64,2048]{4,3,2,1,0:T(8,128)(2,1)S(1)}, bf16[1,2,2,64,2048]{4,3,2,1,0:T(8,128)(2,1)}, u32[]{:S(2)}) copy-start(bf16[1,2,2,64,2048]{4,3,2,1,0:T(8,128)(2,1)} %recorded_ref.1) | copy-start | bytes 3145732
  7.8 19.1 %copy-start.1 = (s32[256]{0:T(256)S(1)}, s32[256]{0:T(256)}, u32[]{:S(2)}) copy-start(s32[256]{0:T(256)} %param.12) | copy-start | bytes 3076
  7.8 19.1 %copy-start.2 = (s32[4]{0:T(128)S(1)}, s32[4]{0:T(128)}, u32[]{:S(2)}) copy-start(s32[4]{0:T(128)} %owner_ref.1) | copy-start | bytes 52
  7.9 44.2 %copy-start.4 = (s32[512]{0:T(512)S(1)}, s32[512]{0:T(512)}, u32[]{:S(2)}) copy-start(s32[512]{0:T(512)} %param.10) | copy-start | bytes 6148
  7.9 44.2 %copy-start.5 = (s32[512]{0:T(512)S(1)}, s32[512]{0:T(512)}, u32[]{:S(2)}) copy-start(s32[512]{0:T(512)} %param.11) | copy-start | bytes 6148
  7.9 44.2 %copy-start.6 = (f32[8]{0:T(128)S(1)}, f32[8]{0:T(128)}, u32[]{:S(2)}) copy-start(f32[8]{0:T(128)} %refs_8_.1) | copy-start | bytes 100
  28.3 19.3 %all-to-all-start.1 = ((bf16[4,272,256]{2,1,0:T(8,128)(2,1)}), bf16[4,272,256]{2,1,0:T(8,128)(2,1)S(1)}, u32[]{:S(2)}, u32[]{:S(2)}) async-start(bf16[4,272,256]{2,1,0:T(8,128)(2,1)} %pick.1), calls=%async_computation.1 | async-start | bytes 1114112 | tf_op jit(solution)/shard_map/all_to_all | solution.py:138
  31.8 33.7 %collective-permute-start.5 = (bf16[2,2,512,256]{3,2,1,0:T(8,128)(2,1)S(1)}, bf16[2,2,512,256]{3,2,1,0:T(8,128)(2,1)}, u32[]{:S(2)}, u32[]{:S(2)}) collective-permute-start(bf16[2,2,512,256]{3,2,1,0:T(8,128)(2,1)S(1)} %collective-permute-done.refs_0_), channel_id=1, source_target_pairs={{1,0},{2,3},{5,4},{6,7},{9,8},{10,11},{13,12},{14,15},{17,16},{18,... | collective-permute-start | bytes 3145736 | tf_op jit(solution)/shard_map/ppermute | solution.py:26
  34.2 17.3 %collective-permute-start.2 = (bf16[2,512,256]{2,1,0:T(8,128)(2,1)}, bf16[2,512,256]{2,1,0:T(8,128)(2,1)S(1)}, u32[]{:S(2)}, u32[]{:S(2)}) collective-permute-start(bf16[2,512,256]{2,1,0:T(8,128)(2,1)} %get-tuple-element.26), channel_id=1, source_target_pairs={{2,1},{1,2},{6,5},{5,6},{10,9},{9,10},{14,13},{13,14},{18,17},{17,... | collective-permute-start | bytes 1572872 | tf_op jit(solution)/shard_map/ppermute | solution.py:26
  47.9 19.0 %collective-permute-start.10 = (bf16[256,1024]{1,0:T(8,128)(2,1)S(1)}, bf16[256,1024]{1,0:T(8,128)(2,1)S(1)}, u32[]{:S(2)}, u32[]{:S(2)}) collective-permute-start(bf16[256,1024]{1,0:T(8,128)(2,1)S(1)} %get-tuple-element.33.refs_0_), channel_id=1, source_target_pairs={{24,0},{28,4},{16,8},{20,12},{8,16},{12,20},{0,24},{4,28},{25,1},{... | collective-permute-start | bytes 1572872 | tf_op jit(solution)/shard_map/ppermute | solution.py:26
  49.1 21.9 %collective-permute-start.8 = (bf16[256,1024]{1,0:T(8,128)(2,1)S(1)}, bf16[256,1024]{1,0:T(8,128)(2,1)S(1)}, u32[]{:S(2)}, u32[]{:S(2)}) collective-permute-start(bf16[256,1024]{1,0:T(8,128)(2,1)S(1)} %get-tuple-element.33.refs_0_), channel_id=1, source_target_pairs={{8,0},{12,4},{0,8},{4,12},{24,16},{28,20},{16,24},{20,28},{9,1},{1... | collective-permute-start | bytes 1572872 | tf_op jit(solution)/shard_map/ppermute | solution.py:26
  50.0 21.9 %collective-permute-start.9 = (bf16[256,1024]{1,0:T(8,128)(2,1)S(1)}, bf16[256,1024]{1,0:T(8,128)(2,1)S(1)}, u32[]{:S(2)}, u32[]{:S(2)}) collective-permute-start(bf16[256,1024]{1,0:T(8,128)(2,1)S(1)} %get-tuple-element.33.refs_0_), channel_id=1, source_target_pairs={{16,0},{20,4},{24,8},{28,12},{0,16},{4,20},{8,24},{12,28},{17,1},{... | collective-permute-start | bytes 1572872 | tf_op jit(solution)/shard_map/ppermute | solution.py:26
  51.4 21.0 %collective-permute-start.3 = (bf16[2,512,256]{2,1,0:T(8,128)(2,1)}, bf16[2,512,256]{2,1,0:T(8,128)(2,1)S(1)}, u32[]{:S(2)}, u32[]{:S(2)}) collective-permute-start(bf16[2,512,256]{2,1,0:T(8,128)(2,1)} %get-tuple-element.27), channel_id=1, source_target_pairs={{2,1},{1,2},{6,5},{5,6},{10,9},{9,10},{14,13},{13,14},{18,17},{17,... | collective-permute-start | bytes 1572872 | tf_op jit(solution)/shard_map/ppermute | solution.py:26
  52.1 1.2 %copy-start.3 = (bf16[2,2,512,256]{3,2,1,0:T(8,128)(2,1)S(1)}, bf16[2,2,512,256]{3,2,1,0:T(8,128)(2,1)}, u32[]{:S(2)}) copy-start(bf16[2,2,512,256]{3,2,1,0:T(8,128)(2,1)} %refs_0_.1) | copy-start | bytes 3145732
  65.5 14.3 %collective-permute-start.6 = (bf16[2,512,256]{2,1,0:T(8,128)(2,1)S(1)}, bf16[2,512,256]{2,1,0:T(8,128)(2,1)S(1)}, u32[]{:S(2)}, u32[]{:S(2)}) collective-permute-start(bf16[2,512,256]{2,1,0:T(8,128)(2,1)S(1)} %collective-permute-done.2.refs_14_), channel_id=1, source_target_pairs={{1,0},{2,3},{5,4},{6,7},{9,8},{10,11},{13,12},{14,15},{17,16},{18,... | collective-permute-start | bytes 1572872 | tf_op jit(solution)/shard_map/ppermute | solution.py:26
  66.8 14.3 %collective-permute-start.7 = (bf16[256,1024]{1,0:T(8,128)(2,1)S(1)}, bf16[256,1024]{1,0:T(8,128)(2,1)S(1)}, u32[]{:S(2)}, u32[]{:S(2)}) collective-permute-start(bf16[256,1024]{1,0:T(8,128)(2,1)S(1)} %get-tuple-element.33.refs_0_), channel_id=1, source_target_pairs={{4,0},{0,4},{12,8},{8,12},{20,16},{16,20},{28,24},{24,28},{5,1},{1... | collective-permute-start | bytes 1572872 | tf_op jit(solution)/shard_map/ppermute | solution.py:26
  71.9 9.2 %collective-permute-start.11 = (bf16[256,1024]{1,0:T(8,128)(2,1)S(1)}, bf16[256,1024]{1,0:T(8,128)(2,1)S(1)}, u32[]{:S(2)}, u32[]{:S(2)}) collective-permute-start(bf16[256,1024]{1,0:T(8,128)(2,1)S(1)} %collective-permute-done.8.refs_2_), channel_id=1, source_target_pairs={{4,0},{0,4},{12,8},{8,12},{20,16},{16,20},{28,24},{24,28},{5,1},{1... | collective-permute-start | bytes 1572872 | tf_op jit(solution)/shard_map/ppermute | solution.py:26
  71.9 9.2 %collective-permute-start.12 = (bf16[256,1024]{1,0:T(8,128)(2,1)S(1)}, bf16[256,1024]{1,0:T(8,128)(2,1)S(1)}, u32[]{:S(2)}, u32[]{:S(2)}) collective-permute-start(bf16[256,1024]{1,0:T(8,128)(2,1)S(1)} %collective-permute-done.9.refs_4_), channel_id=1, source_target_pairs={{4,0},{0,4},{12,8},{8,12},{20,16},{16,20},{28,24},{24,28},{5,1},{1... | collective-permute-start | bytes 1572872 | tf_op jit(solution)/shard_map/ppermute | solution.py:26
  72.4 8.7 %collective-permute-start.13 = (bf16[256,1024]{1,0:T(8,128)(2,1)S(1)}, bf16[256,1024]{1,0:T(8,128)(2,1)S(1)}, u32[]{:S(2)}, u32[]{:S(2)}) collective-permute-start(bf16[256,1024]{1,0:T(8,128)(2,1)S(1)} %collective-permute-done.10.refs_6_), channel_id=1, source_target_pairs={{4,0},{0,4},{12,8},{8,12},{20,16},{16,20},{28,24},{24,28},{5,1},{1... | collective-permute-start | bytes 1572872 | tf_op jit(solution)/shard_map/ppermute | solution.py:26
  79.8 13.4 %collective-permute-start.4 = (bf16[2,512,256]{2,1,0:T(8,128)(2,1)S(1)}, bf16[2,512,256]{2,1,0:T(8,128)(2,1)S(1)}, u32[]{:S(2)}, u32[]{:S(2)}) collective-permute-start(bf16[2,512,256]{2,1,0:T(8,128)(2,1)S(1)} %collective-permute-done.3.refs_16_), channel_id=1, source_target_pairs={{1,0},{2,3},{5,4},{6,7},{9,8},{10,11},{13,12},{14,15},{17,16},{18,... | collective-permute-start | bytes 1572872 | tf_op jit(solution)/shard_map/ppermute | solution.py:26

commit v5 on v4

--- a/solution.py
+++ b/solution.py
@@ -11,9 +11,9 @@
 EDGE = 64
 LANES = 128
 LABEL_ROWS = 16
-PICK_FLOPS = 0 * 10**9
+PICK_FLOPS = 0
 TAPER_FLOPS = 10**9
-SUM_FLOPS = 4 * 10**9
+SUM_FLOPS = 12 * 10**9
 LAST_FLOPS = 10**9
 ROWS_BY_ROWS = (((1,), (1,)), ((), ()))
 WHOLE = pl.BlockSpec(memory_space=pltpu.VMEM)
@@ -318,48 +318,40 @@
         labels,
     )
 
-    if bins == 4:
-        inner, outward = [(1, 2), (2, 1)], [(1, 0), (2, 3)]
-        near = exchange(local_gathers, "rbin", 1)
-        across = exchange(local_gathers, "rbin", 3, inner)
-        second = exchange(across, "rbin", 1, outward)
-        units = taper([0, 1], [local_gathers, near], taper_args)
-        over, down, corner = [exchange(piece, "shot", d) for d in (2, 4, 6)]
-        beside = exchange(piece, "shot", 1)
-        first = exchange(after(near[0], across), "rbin", 3, inner)
-        near_1 = after(near[1], first)
-        first_g, second, units = lax.optimization_barrier((first, second, units))
-        passed_0 = exchange(first_g, "rbin", 1, outward)
-        other = exchange(near_1, "rbin", 3, inner)
-        over, down, corner = lax.optimization_barrier((over, down, corner))
-        passed_1 = exchange(other, "rbin", 1, outward)
-        pieces = [[piece], [beside]]
-        for value in (over, down, corner):
-            pieces += [[value], [exchange(value, "shot", 1)]]
-        gathers = [
-            [[units[0]], [units[1]], [first, second], [across, passed_0]],
-            [[units[0]], [units[1]], [other, second], [across, passed_1]],
-        ]
-        pieces[0] = [after(piece, passed_0)]
-        return product(pieces, gathers, [2], taper_args)
-    else:
-        raw = [local_gathers] + [exchange(local_gathers, "rbin", d) for d in range(1, bins)]
-        units = [taper([d], [raw[d]], taper_args)[0] for d in range(bins - 1)] + [raw[-1]]
-        gathers = [[[unit] for unit in units]] * freqs
-        raw_units = []
-
-    if slots == 8:
-        half = piece.shape[0] // 2
-        over = exchange(piece, "shot", 2)
-        down = exchange(piece, "shot", 4)
-        corner = [exchange(over[:half], "shot", 4), exchange(down[half:], "shot", 2)]
-        pieces = {0: [piece], 2: [over], 4: [down], 6: corner}
-    else:
-        pieces = {d: [exchange(piece, "shot", d) if d else piece] for d in range(0, slots, 2)}
+    if (bins, slots, freqs) == (4, 8, 2):
+        return short_way(local_gathers, piece, taper_args)
+    raw = [local_gathers] + [exchange(local_gathers, "rbin", d) for d in range(1, bins)]
+    units = [taper([d], [raw[d]], taper_args)[0] for d in range(bins - 1)] + [raw[-1]]
+    pieces = []
     for d in range(0, slots, 2):
-        pieces[d + 1] = [exchange(p, "shot", 1) for p in pieces[d]]
-    pieces = [pieces[d] for d in range(slots)]
-    return product(pieces, gathers, raw_units, taper_args)
+        value = exchange(piece, "shot", d) if d else piece
+        pieces += [[value], [exchange(value, "shot", 1)]]
+    return product(pieces, [[[unit] for unit in units]] * freqs, [], taper_args)
+
+
+def short_way(local_gathers, piece, taper_args):
+    inner, outward = [(1, 2), (2, 1)], [(1, 0), (2, 3)]
+    near = exchange(local_gathers, "rbin", 1)
+    across = exchange(local_gathers, "rbin", 3, inner)
+    second = exchange(across, "rbin", 1, outward)
+    units = taper([0, 1], [local_gathers, near], taper_args)
+    over, down, corner = [exchange(piece, "shot", d) for d in (2, 4, 6)]
+    beside = exchange(piece, "shot", 1)
+    crossed_0 = exchange(after(near[0], across), "rbin", 3, inner)
+    near_1 = after(near[1], crossed_0)
+    to_pass, second, units, beside = lax.optimization_barrier((crossed_0, second, units, beside))
+    passed_0 = exchange(to_pass, "rbin", 1, outward)
+    crossed_1 = exchange(near_1, "rbin", 3, inner)
+    over, down, corner = lax.optimization_barrier((over, down, corner))
+    passed_1 = exchange(crossed_1, "rbin", 1, outward)
+    pieces = [[after(piece, passed_0)], [beside]]
+    for value in (over, down, corner):
+        pieces += [[value], [exchange(value, "shot", 1)]]
+    gathers = [
+        [[units[0]], [units[1]], [crossed_0, second], [across, passed_0]],
+        [[units[0]], [units[1]], [crossed_1, second], [across, passed_1]],
+    ]
+    return product(pieces, gathers, [2], taper_args)
 
 
 def solution(mesh):

time: 95.6 us -> 94.1 us (0.984)
  waiting for transfers between devices: 39.4 us -> 38.2 us
    ppermute x14, waiting for transfers between devices: 26.6 us -> 25.3 us  [exchange(): lax.ppermute(value, axis, [p for p in pairs if among is None or p in among])]
    unnamed x14 -> x16, local copies, waits for them, and re-layouts: 2.47 us -> 2.47 us
where the time goes in v5:
time: 94.1 us; the launch traced here: 93.7 us
  waiting for transfers between devices  38.2 us (41%)
  starting transfers between devices  19.4 us (21%)
  blocking collectives  19 us (20%)
  Pallas kernels  13.4 us (14%)
  local copies, waits for them, and re-layouts  3.49 us (4%)
    ppermute x14, waiting for transfers between devices, exchange(): lax.ppermute(value, axis, [p for p in pairs if among is None or p in among])  25.3 us
    all_to_all x1, blocking collectives, wanted_shares(): shares = lax.all_to_all(shares, 'shot', 0, 0)  19 us
    ppermute x14, starting transfers between devices, exchange(): lax.ppermute(value, axis, [p for p in pairs if among is None or p in among])  15.9 us
    all_to_all x1, waiting for transfers between devices, wanted_shares(): return turn(lax.all_to_all(picked, 'rbin', 0, 0), points)  12.8 us
    pallas_call x1, Pallas kernels, product(): pl.pallas_call(functools.partial(sum_kernel, freqs, order, raw_units, len...  6.2 us
    pallas_call x2, Pallas kernels, product(): pl.pallas_call(functools.partial(last_kernel, bins, freq, n), in_specs=[W...  3.86 us
    all_to_all x1, starting transfers between devices, wanted_shares(): return turn(lax.all_to_all(picked, 'rbin', 0, 0), points)  3.47 us
    unnamed x16, local copies, waits for them, and re-layouts  2.47 us
  transfers between devices with their start and end apart: 15, of which 6 were waited for; matrix products, arithmetic and copies ran while one was open for 1% of the time, Pallas kernels for 12%

profile of v5, /device:TPU:0, one launch (start us, length us, event | category | flops | bytes accessed | tf_op | source)
XLA Modules:
  0.0 93.7 jit_solution(231682573685030272)
XLA Ops:
  0.0 0.7 collective-permute-start
  0.7 5.8 %collective-permute-start.1 = (bf16[2,2,512,256]{3,2,1,0:T(8,128)(2,1)}, bf16[2,2,512,256]{3,2,1,0:T(8,128)(2,1)S(1)}, u32[]{:S(2)}, u32[]{:S(2)}) collective-permute-start(bf16[2,2,512,256]{3,2,1,0:T(8,128)(2,1)} %refs_0_.1), channel_id=1, source_target_pairs={{1,0},{0,1},{3,2},{2,3},{5,4},{4,5},{7,6},{6,7},{9,8},{8,9},{11,10... | collective-permute-start | bytes 3145736 | tf_op jit(solution)/shard_map/ppermute | solution.py:26
  6.6 1.2 %copy-done = bf16[1,2,2,64,2048]{4,3,2,1,0:T(8,128)(2,1)S(1)} copy-done((bf16[1,2,2,64,2048]{4,3,2,1,0:T(8,128)(2,1)S(1)}, bf16[1,2,2,64,2048]{4,3,2,1,0:T(8,128)(2,1)}, u32[]{:S(2)}) %copy-start) | copy-done | bytes 1048600
  7.8 0.1 share.1
  7.9 0.0 copy-start.4
  7.9 0.0 copy-start.5
  7.9 0.0 copy-start.6
  7.9 19.0 %all_to_all.10.shares_ref = bf16[8,64,1024]{2,1,0:T(8,128)(2,1)S(1)} all-to-all(bf16[8,64,1024]{2,1,0:T(8,128)(2,1)S(1)} %share.1), channel_id=1, replica_groups=mesh['shot'=8,'rbin'=4] {'shot'}, dimensions={0} | all-to-all | bytes 2097152 | tf_op jit(solution)/shard_map/all_to_all | solution.py:129
  26.9 0.0 copy-done.1
  26.9 0.0 copy-done.2
  26.9 1.4 %pick.1 = bf16[4,272,256]{2,1,0:T(8,128)(2,1)} custom-call(s32[4]{0:T(128)S(1)} %copy-done.2, s32[1,256]{1,0:T(1,128)S(1)} %bitcast.7, bf16[8,64,1024]{2,1,0:T(8,128)(2,1)S(1)} %all_to_all.10.shares_ref), custom_call_target="tpu_custom_call" | custom-call | bytes 2097152 | tf_op jit(solution)/shard_map/pick/pallas_call | solution.py:130
  28.3 3.5 %all-to-all-start.1 = ((bf16[4,272,256]{2,1,0:T(8,128)(2,1)}), bf16[4,272,256]{2,1,0:T(8,128)(2,1)S(1)}, u32[]{:S(2)}, u32[]{:S(2)}) async-start(bf16[4,272,256]{2,1,0:T(8,128)(2,1)} %pick.1), calls=%async_computation.1 | async-start | bytes 1114112 | tf_op jit(solution)/shard_map/all_to_all | solution.py:138
  31.8 0.0 collective-permute-done.refs_0_
  31.8 1.3 %collective-permute-start.5 = (bf16[2,2,512,256]{3,2,1,0:T(8,128)(2,1)S(1)}, bf16[2,2,512,256]{3,2,1,0:T(8,128)(2,1)}, u32[]{:S(2)}, u32[]{:S(2)}) collective-permute-start(bf16[2,2,512,256]{3,2,1,0:T(8,128)(2,1)S(1)} %collective-permute-done.refs_0_), channel_id=1, source_target_pairs={{1,0},{2,3},{5,4},{6,7},{9,8},{10,11},{13,12},{14,15},{17,16},{18,... | collective-permute-start | bytes 3145736 | tf_op jit(solution)/shard_map/ppermute | solution.py:26
  33.1 0.0 collective-permute-done.1.refs_1_
  33.1 1.0 %slice_bitcast_fusion = (bf16[2,512,256]{2,1,0:T(8,128)(2,1)}, bf16[2,512,256]{2,1,0:T(8,128)(2,1)}) fusion(bf16[2,2,512,256]{3,2,1,0:T(8,128)(2,1)S(1)} %collective-permute-done.1.refs_1_), kind=kLoop, calls=%fused_computation | loop fusion | bytes 2097152 | tf_op jit(solution)/shard_map/squeeze | solution.py:340
  34.1 0.7 collective-permute-start.2
  34.8 12.8 %all-to-all-done.1.picked_ref = bf16[4,272,256]{2,1,0:T(8,128)(2,1)S(1)} async-done(((bf16[4,272,256]{2,1,0:T(8,128)(2,1)}), bf16[4,272,256]{2,1,0:T(8,128)(2,1)S(1)}, u32[]{:S(2)}, u32[]{:S(2)}) %all-to-all-start.1) | async-done | bytes 557088 | tf_op jit(solution)/shard_map/all_to_all | solution.py:138
  47.7 0.2 turn.1
  47.9 0.1 collective-permute-start.6
  47.9 1.2 %collective-permute-start.10 = (bf16[256,1024]{1,0:T(8,128)(2,1)S(1)}, bf16[256,1024]{1,0:T(8,128)(2,1)S(1)}, u32[]{:S(2)}, u32[]{:S(2)}) collective-permute-start(bf16[256,1024]{1,0:T(8,128)(2,1)S(1)} %get-tuple-element.34.refs_0_), channel_id=1, source_target_pairs={{24,0},{28,4},{16,8},{20,12},{8,16},{12,20},{0,24},{4,28},{25,1},{... | collective-permute-start | bytes 1572872 | tf_op jit(solution)/shard_map/ppermute | solution.py:26
  49.1 0.9 collective-permute-start.8
  50.0 0.0 collective-permute-done.2.refs_14_
  50.0 1.5 %collective-permute-start.9 = (bf16[256,1024]{1,0:T(8,128)(2,1)S(1)}, bf16[256,1024]{1,0:T(8,128)(2,1)S(1)}, u32[]{:S(2)}, u32[]{:S(2)}) collective-permute-start(bf16[256,1024]{1,0:T(8,128)(2,1)S(1)} %get-tuple-element.34.refs_0_), channel_id=1, source_target_pairs={{16,0},{20,4},{24,8},{28,12},{0,16},{4,20},{8,24},{12,28},{17,1},{... | collective-permute-start | bytes 1572872 | tf_op jit(solution)/shard_map/ppermute | solution.py:26
  51.5 0.0 copy-done.4
  51.5 0.0 copy-done.5
  51.5 1.2 %copy-done.3 = bf16[2,2,512,256]{3,2,1,0:T(8,128)(2,1)S(1)} copy-done((bf16[2,2,512,256]{3,2,1,0:T(8,128)(2,1)S(1)}, bf16[2,2,512,256]{3,2,1,0:T(8,128)(2,1)}, u32[]{:S(2)}) %copy-start.3) | copy-done | bytes 1048600
  52.7 1.7 %taper.1 = (bf16[2,2,512,256]{3,2,1,0:T(8,128)(2,1)S(1)}, bf16[2,2,512,256]{3,2,1,0:T(8,128)(2,1)S(1)}) custom-call(f32[8]{0:T(128)S(1)} %copy-done.6, s32[1,512]{1,0:T(1,128)S(1)} %bitcast.8, s32[1,512]{1,0:T(1,128)S(1)} %bitcast.10, f32[4,256]{1,0:T(4,128)S(1)} %get-tuple-element.30.bins_ref.refs_11_, bf16[2,2,512,256]{3,2,1,0:T(8,128)(2,1)S(1)} %copy-done.3, ...), custom_call_target="tpu_custom_call" | custom-call | flops 1000000000 | bytes 2097152 | tf_op jit(solution)/shard_map/taper/pallas_call | solution.py:71
  54.4 11.1 %collective-permute-done.5.refs_15_ = bf16[2,2,512,256]{3,2,1,0:T(8,128)(2,1)} collective-permute-done((bf16[2,2,512,256]{3,2,1,0:T(8,128)(2,1)S(1)}, bf16[2,2,512,256]{3,2,1,0:T(8,128)(2,1)}, u32[]{:S(2)}, u32[]{:S(2)}) %collective-permute-start.5) | collective-permute-done | bytes 1048608 | tf_op jit(solution)/shard_map/ppermute | solution.py:26
  65.5 0.7 collective-permute-start.3
  66.2 0.0 collective-permute-done.6.refs_1_
  66.2 1.3 %collective-permute-start.7 = (bf16[2,512,256]{2,1,0:T(8,128)(2,1)S(1)}, bf16[2,512,256]{2,1,0:T(8,128)(2,1)S(1)}, u32[]{:S(2)}, u32[]{:S(2)}) collective-permute-start(bf16[2,512,256]{2,1,0:T(8,128)(2,1)S(1)} %collective-permute-done.2.refs_14_), channel_id=1, source_target_pairs={{1,0},{2,3},{5,4},{6,7},{9,8},{10,11},{13,12},{14,15},{17,16},{18,... | collective-permute-start | bytes 1572872 | tf_op jit(solution)/shard_map/ppermute | solution.py:26
  67.5 0.0 collective-permute-done.10.refs_6_
  67.5 6.0 %collective-permute-done.8.refs_2_ = bf16[256,1024]{1,0:T(8,128)(2,1)S(1)} collective-permute-done((bf16[256,1024]{1,0:T(8,128)(2,1)S(1)}, bf16[256,1024]{1,0:T(8,128)(2,1)S(1)}, u32[]{:S(2)}, u32[]{:S(2)}) %collective-permute-start.8) | collective-permute-done | bytes 524320 | tf_op jit(solution)/shard_map/ppermute | solution.py:26
  73.6 0.9 collective-permute-done.9.refs_4_
  74.4 0.0 collective-permute-start.11
  74.4 0.5 collective-permute-start.12
  74.9 0.0 collective-permute-start.13
  74.9 0.0 collective-permute-done.3.refs_16_
  74.9 1.3 %collective-permute-start.4 = (bf16[2,512,256]{2,1,0:T(8,128)(2,1)S(1)}, bf16[2,512,256]{2,1,0:T(8,128)(2,1)S(1)}, u32[]{:S(2)}, u32[]{:S(2)}) collective-permute-start(bf16[2,512,256]{2,1,0:T(8,128)(2,1)S(1)} %collective-permute-done.3.refs_16_), channel_id=1, source_target_pairs={{1,0},{2,3},{5,4},{6,7},{9,8},{10,11},{13,12},{14,15},{17,16},{18,... | collective-permute-start | bytes 1572872 | tf_op jit(solution)/shard_map/ppermute | solution.py:26
  76.2 4.8 %collective-permute-done.7.refs_1_ = bf16[2,512,256]{2,1,0:T(8,128)(2,1)S(1)} collective-permute-done((bf16[2,512,256]{2,1,0:T(8,128)(2,1)S(1)}, bf16[2,512,256]{2,1,0:T(8,128)(2,1)S(1)}, u32[]{:S(2)}, u32[]{:S(2)}) %collective-permute-start.7) | collective-permute-done | bytes 524320 | tf_op jit(solution)/shard_map/ppermute | solution.py:26
  81.0 0.0 collective-permute-done.11.refs_3_
  81.0 0.0 collective-permute-done.12.refs_5_
  81.0 0.0 collective-permute-done.13.refs_7_
  81.1 6.2 %sum.1 = (f32[512,512]{1,0:T(8,128)S(1)}, f32[512,512]{1,0:T(8,128)S(1)}, bf16[2,512,256]{2,1,0:T(8,128)(2,1)S(1)}, f32[512,512]{1,0:T(8,128)S(1)}, f32[512,512]...) custom-call(bf16[256,1024]{1,0:T(8,128)(2,1)S(1)} %get-tuple-element.34.refs_0_, ...), custom_call_target="tpu_custom_call" | custom-call | flops 12000000000 | bytes 2097152 | tf_op jit(solution)/shard_map/sum/pallas_call | solution.py:271
  87.3 1.9 %last.2.refs_6_ = f32[2,512,2,512]{3,2,1,0:T(2,128)} custom-call(bf16[2,2,512,256]{3,2,1,0:T(8,128)(2,1)S(1)} %collective-permute-done.refs_0_, bf16[2,512,256]{2,1,0:T(8,128)(2,1)S(1)} %collective-permute-done.7.refs_1_, f32[512,512]{1,0:T(8,128)S(1)} %get-tuple-element.46.refs_2_, f32[512,512]{1,0:T(8,128)S(1)} %get-tuple-element.47.refs_3_, ...), custom_call_target="tpu_custom_call" | custom-call | flops 1000000000 | bytes 2097152 | tf_op jit(solution)/shard_map/last/pallas_call | solution.py:290
  89.2 2.5 %collective-permute-done.4.refs_1_ = bf16[2,512,256]{2,1,0:T(8,128)(2,1)S(1)} collective-permute-done((bf16[2,512,256]{2,1,0:T(8,128)(2,1)S(1)}, bf16[2,512,256]{2,1,0:T(8,128)(2,1)S(1)}, u32[]{:S(2)}, u32[]{:S(2)}) %collective-permute-start.4) | collective-permute-done | bytes 524320 | tf_op jit(solution)/shard_map/ppermute | solution.py:26
  91.8 1.9 %last.3 = f32[2,512,2,512]{3,2,1,0:T(2,128)} custom-call(bf16[2,2,512,256]{3,2,1,0:T(8,128)(2,1)S(1)} %collective-permute-done.refs_0_, bf16[2,512,256]{2,1,0:T(8,128)(2,1)S(1)} %collective-permute-done.4.refs_1_, f32[512,512]{1,0:T(8,128)S(1)} %get-tuple-element.42.refs_2_, ...), custom_call_target="tpu_custom_call", output_to_operand_aliasing={{}: (6, {})} | custom-call | flops 1000000000 | bytes 2097152 | tf_op jit(solution)/shard_map/last/pallas_call | solution.py:290
  (7 shorter events, 0.0 us)
Async XLA Ops:
  0.0 31.8 %collective-permute-start = (bf16[2,2,512,256]{3,2,1,0:T(8,128)(2,1)}, bf16[2,2,512,256]{3,2,1,0:T(8,128)(2,1)S(1)}, u32[]{:S(2)}, u32[]{:S(2)}) collective-permute-start(bf16[2,2,512,256]{3,2,1,0:T(8,128)(2,1)} %refs_0_.1), channel_id=1, source_target_pairs={{2,1},{1,2},{6,5},{5,6},{10,9},{9,10},{14,13},{13,14},{18,17},{17,... | collective-permute-start | bytes 3145736 | tf_op jit(solution)/shard_map/ppermute | solution.py:26
  0.7 32.4 %collective-permute-start.1 = (bf16[2,2,512,256]{3,2,1,0:T(8,128)(2,1)}, bf16[2,2,512,256]{3,2,1,0:T(8,128)(2,1)S(1)}, u32[]{:S(2)}, u32[]{:S(2)}) collective-permute-start(bf16[2,2,512,256]{3,2,1,0:T(8,128)(2,1)} %refs_0_.1), channel_id=1, source_target_pairs={{1,0},{0,1},{3,2},{2,3},{5,4},{4,5},{7,6},{6,7},{9,8},{8,9},{11,10... | collective-permute-start | bytes 3145736 | tf_op jit(solution)/shard_map/ppermute | solution.py:26
  6.6 1.2 %copy-start = (bf16[1,2,2,64,2048]{4,3,2,1,0:T(8,128)(2,1)S(1)}, bf16[1,2,2,64,2048]{4,3,2,1,0:T(8,128)(2,1)}, u32[]{:S(2)}) copy-start(bf16[1,2,2,64,2048]{4,3,2,1,0:T(8,128)(2,1)} %recorded_ref.1) | copy-start | bytes 3145732
  7.8 19.1 %copy-start.1 = (s32[256]{0:T(256)S(1)}, s32[256]{0:T(256)}, u32[]{:S(2)}) copy-start(s32[256]{0:T(256)} %param.12) | copy-start | bytes 3076
  7.8 19.1 %copy-start.2 = (s32[4]{0:T(128)S(1)}, s32[4]{0:T(128)}, u32[]{:S(2)}) copy-start(s32[4]{0:T(128)} %owner_ref.1) | copy-start | bytes 52
  7.9 43.6 %copy-start.4 = (s32[512]{0:T(512)S(1)}, s32[512]{0:T(512)}, u32[]{:S(2)}) copy-start(s32[512]{0:T(512)} %param.10) | copy-start | bytes 6148
  7.9 43.6 %copy-start.5 = (s32[512]{0:T(512)S(1)}, s32[512]{0:T(512)}, u32[]{:S(2)}) copy-start(s32[512]{0:T(512)} %param.11) | copy-start | bytes 6148
  7.9 43.6 %copy-start.6 = (f32[8]{0:T(128)S(1)}, f32[8]{0:T(128)}, u32[]{:S(2)}) copy-start(f32[8]{0:T(128)} %refs_8_.1) | copy-start | bytes 100
  28.3 19.3 %all-to-all-start.1 = ((bf16[4,272,256]{2,1,0:T(8,128)(2,1)}), bf16[4,272,256]{2,1,0:T(8,128)(2,1)S(1)}, u32[]{:S(2)}, u32[]{:S(2)}) async-start(bf16[4,272,256]{2,1,0:T(8,128)(2,1)} %pick.1), calls=%async_computation.1 | async-start | bytes 1114112 | tf_op jit(solution)/shard_map/all_to_all | solution.py:138
  31.8 33.7 %collective-permute-start.5 = (bf16[2,2,512,256]{3,2,1,0:T(8,128)(2,1)S(1)}, bf16[2,2,512,256]{3,2,1,0:T(8,128)(2,1)}, u32[]{:S(2)}, u32[]{:S(2)}) collective-permute-start(bf16[2,2,512,256]{3,2,1,0:T(8,128)(2,1)S(1)} %collective-permute-done.refs_0_), channel_id=1, source_target_pairs={{1,0},{2,3},{5,4},{6,7},{9,8},{10,11},{13,12},{14,15},{17,16},{18,... | collective-permute-start | bytes 3145736 | tf_op jit(solution)/shard_map/ppermute | solution.py:26
  34.1 15.9 %collective-permute-start.2 = (bf16[2,512,256]{2,1,0:T(8,128)(2,1)}, bf16[2,512,256]{2,1,0:T(8,128)(2,1)S(1)}, u32[]{:S(2)}, u32[]{:S(2)}) collective-permute-start(bf16[2,512,256]{2,1,0:T(8,128)(2,1)} %get-tuple-element.27), channel_id=1, source_target_pairs={{2,1},{1,2},{6,5},{5,6},{10,9},{9,10},{14,13},{13,14},{18,17},{17,... | collective-permute-start | bytes 1572872 | tf_op jit(solution)/shard_map/ppermute | solution.py:26
  47.7 17.9 %copy-start.7 = (bf16[2,512,256]{2,1,0:T(8,128)(2,1)S(1)}, bf16[2,512,256]{2,1,0:T(8,128)(2,1)}, u32[]{:S(2)}) copy-start(bf16[2,512,256]{2,1,0:T(8,128)(2,1)} %get-tuple-element.28) | copy-start | bytes 1572868
  47.9 18.4 %collective-permute-start.6 = (bf16[256,1024]{1,0:T(8,128)(2,1)S(1)}, bf16[256,1024]{1,0:T(8,128)(2,1)S(1)}, u32[]{:S(2)}, u32[]{:S(2)}) collective-permute-start(bf16[256,1024]{1,0:T(8,128)(2,1)S(1)} %get-tuple-element.34.refs_0_), channel_id=1, source_target_pairs={{4,0},{0,4},{12,8},{8,12},{20,16},{16,20},{28,24},{24,28},{5,1},{1... | collective-permute-start | bytes 1572872 | tf_op jit(solution)/shard_map/ppermute | solution.py:26
  47.9 19.6 %collective-permute-start.10 = (bf16[256,1024]{1,0:T(8,128)(2,1)S(1)}, bf16[256,1024]{1,0:T(8,128)(2,1)S(1)}, u32[]{:S(2)}, u32[]{:S(2)}) collective-permute-start(bf16[256,1024]{1,0:T(8,128)(2,1)S(1)} %get-tuple-element.34.refs_0_), channel_id=1, source_target_pairs={{24,0},{28,4},{16,8},{20,12},{8,16},{12,20},{0,24},{4,28},{25,1},{... | collective-permute-start | bytes 1572872 | tf_op jit(solution)/shard_map/ppermute | solution.py:26
  49.1 24.4 %collective-permute-start.8 = (bf16[256,1024]{1,0:T(8,128)(2,1)S(1)}, bf16[256,1024]{1,0:T(8,128)(2,1)S(1)}, u32[]{:S(2)}, u32[]{:S(2)}) collective-permute-start(bf16[256,1024]{1,0:T(8,128)(2,1)S(1)} %get-tuple-element.34.refs_0_), channel_id=1, source_target_pairs={{8,0},{12,4},{0,8},{4,12},{24,16},{28,20},{16,24},{20,28},{9,1},{1... | collective-permute-start | bytes 1572872 | tf_op jit(solution)/shard_map/ppermute | solution.py:26
  50.0 24.4 %collective-permute-start.9 = (bf16[256,1024]{1,0:T(8,128)(2,1)S(1)}, bf16[256,1024]{1,0:T(8,128)(2,1)S(1)}, u32[]{:S(2)}, u32[]{:S(2)}) collective-permute-start(bf16[256,1024]{1,0:T(8,128)(2,1)S(1)} %get-tuple-element.34.refs_0_), channel_id=1, source_target_pairs={{16,0},{20,4},{24,8},{28,12},{0,16},{4,20},{8,24},{12,28},{17,1},{... | collective-permute-start | bytes 1572872 | tf_op jit(solution)/shard_map/ppermute | solution.py:26
  51.5 1.2 %copy-start.3 = (bf16[2,2,512,256]{3,2,1,0:T(8,128)(2,1)S(1)}, bf16[2,2,512,256]{3,2,1,0:T(8,128)(2,1)}, u32[]{:S(2)}) copy-start(bf16[2,2,512,256]{3,2,1,0:T(8,128)(2,1)} %refs_0_.1) | copy-start | bytes 3145732
  65.5 9.4 %collective-permute-start.3 = (bf16[2,512,256]{2,1,0:T(8,128)(2,1)S(1)}, bf16[2,512,256]{2,1,0:T(8,128)(2,1)S(1)}, u32[]{:S(2)}, u32[]{:S(2)}) collective-permute-start(bf16[2,512,256]{2,1,0:T(8,128)(2,1)S(1)} %copy-done.7), channel_id=1, source_target_pairs={{2,1},{1,2},{6,5},{5,6},{10,9},{9,10},{14,13},{13,14},{18,17},{17,... | collective-permute-start | bytes 1572872 | tf_op jit(solution)/shard_map/ppermute | solution.py:26
  66.2 14.8 %collective-permute-start.7 = (bf16[2,512,256]{2,1,0:T(8,128)(2,1)S(1)}, bf16[2,512,256]{2,1,0:T(8,128)(2,1)S(1)}, u32[]{:S(2)}, u32[]{:S(2)}) collective-permute-start(bf16[2,512,256]{2,1,0:T(8,128)(2,1)S(1)} %collective-permute-done.2.refs_14_), channel_id=1, source_target_pairs={{1,0},{2,3},{5,4},{6,7},{9,8},{10,11},{13,12},{14,15},{17,16},{18,... | collective-permute-start | bytes 1572872 | tf_op jit(solution)/shard_map/ppermute | solution.py:26
  74.4 6.6 %collective-permute-start.11 = (bf16[256,1024]{1,0:T(8,128)(2,1)S(1)}, bf16[256,1024]{1,0:T(8,128)(2,1)S(1)}, u32[]{:S(2)}, u32[]{:S(2)}) collective-permute-start(bf16[256,1024]{1,0:T(8,128)(2,1)S(1)} %collective-permute-done.8.refs_2_), channel_id=1, source_target_pairs={{4,0},{0,4},{12,8},{8,12},{20,16},{16,20},{28,24},{24,28},{5,1},{1... | collective-permute-start | bytes 1572872 | tf_op jit(solution)/shard_map/ppermute | solution.py:26
  74.4 6.6 %collective-permute-start.12 = (bf16[256,1024]{1,0:T(8,128)(2,1)S(1)}, bf16[256,1024]{1,0:T(8,128)(2,1)S(1)}, u32[]{:S(2)}, u32[]{:S(2)}) collective-permute-start(bf16[256,1024]{1,0:T(8,128)(2,1)S(1)} %collective-permute-done.9.refs_4_), channel_id=1, source_target_pairs={{4,0},{0,4},{12,8},{8,12},{20,16},{16,20},{28,24},{24,28},{5,1},{1... | collective-permute-start | bytes 1572872 | tf_op jit(solution)/shard_map/ppermute | solution.py:26
  74.9 6.1 %collective-permute-start.13 = (bf16[256,1024]{1,0:T(8,128)(2,1)S(1)}, bf16[256,1024]{1,0:T(8,128)(2,1)S(1)}, u32[]{:S(2)}, u32[]{:S(2)}) collective-permute-start(bf16[256,1024]{1,0:T(8,128)(2,1)S(1)} %collective-permute-done.10.refs_6_), channel_id=1, source_target_pairs={{4,0},{0,4},{12,8},{8,12},{20,16},{16,20},{28,24},{24,28},{5,1},{1... | collective-permute-start | bytes 1572872 | tf_op jit(solution)/shard_map/ppermute | solution.py:26
  74.9 16.8 %collective-permute-start.4 = (bf16[2,512,256]{2,1,0:T(8,128)(2,1)S(1)}, bf16[2,512,256]{2,1,0:T(8,128)(2,1)S(1)}, u32[]{:S(2)}, u32[]{:S(2)}) collective-permute-start(bf16[2,512,256]{2,1,0:T(8,128)(2,1)S(1)} %collective-permute-done.3.refs_16_), channel_id=1, source_target_pairs={{1,0},{2,3},{5,4},{6,7},{9,8},{10,11},{13,12},{14,15},{17,16},{18,... | collective-permute-start | bytes 1572872 | tf_op jit(solution)/shard_map/ppermute | solution.py:26
